TPU v7x, 32 devices: a whole 2x2x4 slice. The times are simulated.
32 devices in a mesh: row: 4 (over z), col: 8 (over y, x, core).
Axes of the slice: x: 2, y: 2, z: 4, core: 2. Of those that a mesh axis runs over, the one named last changes fastest.
Arguments:
- psi_val: float32 [64, 128, 128, 128], P(None, 'row', 'col'), may hold values from -6 to 6
- psi_cond: float32 [64, 128, 128, 128], P(None, 'row', 'col'), may hold values from -6 to 6
- eps_val: float32 [64], replicated, may hold values from -12 to -1
- eps_cond: float32 [64], replicated, may hold values from 1 to 12
- val_index: int32 [32], replicated, may hold values from 0 to 63
- cond_index: int32 [32], replicated, may hold values from 0 to 63
- gmap: int32 [8192], replicated, may hold values from 0 to 2097151, as said below
- chi0_in: float32 [2, 8192, 8192], P(None, 'row', 'col'), may hold values from -6 to 6
Outputs:
- chi0_out: float32 [2, 8192, 8192], P(None, 'row', 'col')
Inputs may be any that keep to these rules, and one draw needn't show every extreme that they name: gmap holds 8192 distinct entries. Entries g of device block d = g // 256 (d = r * 8 + c) have ky in [r * 32, (r + 1) * 32) and kz in [c * 16, (c + 1) * 16); kx is any.
All inputs are finite; a program needn't handle non-finite values.
Results may differ from a plain program's by a relative error of at most 0.000068.
Values sent between devices are 32-bit elements; how exact they have to be, the bound alone decides.
A program may use at most 256 MiB of HBM per device.

v0:
```python
import math

import jax
import jax.numpy as jnp
from jax import lax
from jax.sharding import PartitionSpec as P

GRID = 128
NG = 8192


HIGH = lax.Precision.HIGHEST


def spread(block, axis, holder):
    block = jnp.where(lax.axis_index(axis) == holder, block, jnp.zeros_like(block))
    return lax.psum(block, axis)


def dft_tables(length):
    steps = jnp.arange(length, dtype=jnp.int32)
    phase = steps[:, None] * steps[None, :] % length
    angle = phase.astype(jnp.float32) * (2.0 * math.pi / length)
    return (jnp.cos(angle), jnp.sin(angle))


def point_tables(freq_x, length):
    steps = jnp.arange(length, dtype=jnp.int32)
    phase = steps[:, None] * freq_x[None, :] % length
    angle = phase.astype(jnp.float32) * (2.0 * math.pi / length)
    return (jnp.cos(angle), jnp.sin(angle))


def pick_points(real_part, imag_part, yz_index, cos_x, sin_x):
    count = real_part.shape[0]
    flat_re = real_part.reshape(count, real_part.shape[1], -1)
    flat_im = imag_part.reshape(count, imag_part.shape[1], -1)
    cols_re = jnp.take(flat_re, yz_index, axis=2)
    cols_im = jnp.take(flat_im, yz_index, axis=2)
    m_re = jnp.sum(cols_re * cos_x[None] + cols_im * sin_x[None], axis=1)
    m_im = jnp.sum(cols_im * cos_x[None] - cols_re * sin_x[None], axis=1)
    return (m_re, m_im)


def contract_pairs(left, right):
    return lax.dot_general(
        left, right, (((0,), (0,)), ((), ())), precision=HIGH, preferred_element_type=jnp.float32
    )


def on_device(psi_val, psi_cond, eps_val, eps_cond, val_index, cond_index, gmap, chi0_in):
    pairs = val_index.shape[0]
    scale = 1.0 / math.sqrt(GRID**3)
    cos_t, sin_t = dft_tables(GRID)
    rho = jnp.take(psi_val, val_index, axis=0) * jnp.take(psi_cond, cond_index, axis=0)
    row_pos = lax.axis_index("row")
    col_pos = lax.axis_index("col")
    mesh_cols = lax.axis_size("col")
    mesh_rows = lax.axis_size("row")
    per_device = NG // (mesh_rows * mesh_cols)
    row_span = GRID // mesh_rows
    col_span = GRID // mesh_cols
    flat_pos = row_pos * mesh_cols + col_pos
    own_map = lax.dynamic_slice_in_dim(gmap, flat_pos * per_device, per_device, 0)
    freq_x = own_map // (GRID * GRID)
    freq_y = own_map // GRID % GRID - row_pos * row_span
    freq_z = own_map % GRID - col_pos * col_span
    yz_index = freq_y * col_span + freq_z
    cos_x, sin_x = point_tables(freq_x, GRID)
    z_re = jnp.einsum("pxyz,zk->pxyk", rho, cos_t, precision=HIGH)
    z_im = -jnp.einsum("pxyz,zk->pxyk", rho, sin_t, precision=HIGH)
    part_re = lax.all_to_all(z_re, "col", split_axis=3, concat_axis=2, tiled=True)
    part_im = lax.all_to_all(z_im, "col", split_axis=3, concat_axis=2, tiled=True)
    y_re = jnp.einsum("pxyz,yk->pxkz", part_re, cos_t, precision=HIGH) + jnp.einsum(
        "pxyz,yk->pxkz", part_im, sin_t, precision=HIGH
    )
    y_im = jnp.einsum("pxyz,yk->pxkz", part_im, cos_t, precision=HIGH) - jnp.einsum(
        "pxyz,yk->pxkz", part_re, sin_t, precision=HIGH
    )
    y_re, y_im = (y_re, y_im)
    m_re, m_im = pick_points(
        lax.all_to_all(y_re, "row", split_axis=2, concat_axis=1, tiled=True),
        lax.all_to_all(y_im, "row", split_axis=2, concat_axis=1, tiled=True),
        yz_index,
        cos_x,
        sin_x,
    )
    m_re = m_re * scale
    m_im = m_im * scale
    cols_span = chi0_in.shape[2]
    rows_re, rows_im = (
        lax.all_gather(m_re, "col", axis=1, tiled=True),
        lax.all_gather(m_im, "col", axis=1, tiled=True),
    )
    offset = col_pos * mesh_rows % mesh_cols * per_device
    piece_re = lax.dynamic_slice_in_dim(rows_re, offset, cols_span, 1)
    piece_im = lax.dynamic_slice_in_dim(rows_im, offset, cols_span, 1)
    root = col_pos * mesh_rows // mesh_cols
    cols_re, cols_im = (spread(piece_re, "row", root), spread(piece_im, "row", root))
    val_hot = val_index[:, None] == jnp.arange(eps_val.shape[0], dtype=jnp.int32)[None, :]
    cond_hot = cond_index[:, None] == jnp.arange(eps_cond.shape[0], dtype=jnp.int32)[None, :]
    energy_v = jnp.sum(jnp.where(val_hot, eps_val[None, :], 0.0), axis=1)
    energy_c = jnp.sum(jnp.where(cond_hot, eps_cond[None, :], 0.0), axis=1)
    weight = (-6.0 / (math.sqrt(pairs) * (energy_c - energy_v)))[:, None]
    out_re = (
        chi0_in[0]
        + contract_pairs(weight * rows_re, cols_re)
        + contract_pairs(weight * rows_im, cols_im)
    )
    out_im = (
        chi0_in[1]
        + contract_pairs(weight * rows_im, cols_re)
        - contract_pairs(weight * rows_re, cols_im)
    )
    return jnp.stack([out_re, out_im])


def solution(mesh):
    return jax.shard_map(
        on_device,
        mesh=mesh,
        in_specs=(
            P(None, "row", "col", None),
            P(None, "row", "col", None),
            P(),
            P(),
            P(),
            P(),
            P(),
            P(None, "row", "col"),
        ),
        out_specs=P(None, "row", "col"),
        check_vma=False,
    )
```

profile of v0, /device:TPU:0, one launch (start us, length us, event | category | flops | bytes accessed | tf_op | source)
XLA Modules:
  0.0 1147.7 jit_solution(7419799512142696927)
XLA Ops:
  6.5 0.7 compare_select_fusion.1
  7.2 0.7 compare_and_fusion.1
  7.9 10.3 gather_fusion.1
  18.2 10.1 gather_fusion
  28.2 13.1 %convolution_negate_fusion = f32[32,32,16,128]{3,2,1,0:T(8,128)} fusion(f32[32,32,16,128]{3,2,1,0:T(8,128)} %gather_fusion.1, f32[32,32,16,128]{3,2,1,0:T(8,128)} %gather_fusion, pred[32]{0:T(512)(128)(4,1)S(1)} %get-tuple-element.17, pred[32]{0:T(512)(128)(4,1)S(1)} %get-tuple-element.18), kind=kOutput, calls=%fused_computation.24 | convolution fusion | flops 3229843456 | bytes 25165888 | tf_op jit(solution)/shard_map/pxyz,zk->pxyk/dot_general | solution.py:71
  41.3 26.3 %copy.59 = f32[32,32,16,128]{1,2,0,3:T(8,128)} copy(f32[32,32,16,128]{3,2,1,0:T(8,128)} %convolution_negate_fusion) | data formatting | bytes 16777216 | tf_op jit(solution)/shard_map/neg | solution.py:71
  67.7 20.5 %reshape.130 = f32[8,1,262144]{2,1,0:T(1,128)} reshape(f32[128,32,16,32]{3,2,1,0:T(8,128)} %bitcast.92) | data formatting | bytes 16777216
  88.2 5.4 all-to-all-start.1
  93.6 13.1 %fusion.34 = f32[32,32,16,128]{3,2,1,0:T(8,128)} fusion(f32[32,32,16,128]{3,2,1,0:T(8,128)} %gather_fusion.1, f32[32,32,16,128]{3,2,1,0:T(8,128)} %gather_fusion, pred[32]{0:T(512)(128)(4,1)S(1)} %get-tuple-element.17, pred[32]{0:T(512)(128)(4,1)S(1)} %get-tuple-element.18), kind=kOutput, calls=%fused_computation.59 | convolution fusion | flops 3227746304 | bytes 25165888 | tf_op jit(solution)/shard_map/pxyz,zk->pxyk/dot_general | solution.py:70
  106.7 26.3 %copy.55 = f32[32,32,16,128]{1,2,0,3:T(8,128)} copy(f32[32,32,16,128]{3,2,1,0:T(8,128)} %fusion.34) | data formatting | bytes 16777216 | tf_op jit(solution)/shard_map/pxyz,zk->pxyk/dot_general | solution.py:70
  133.1 20.5 %reshape.132 = f32[8,1,262144]{2,1,0:T(1,128)} reshape(f32[128,32,16,32]{3,2,1,0:T(8,128)} %bitcast.93) | data formatting | bytes 16777216
  153.6 34.5 %all-to-all-done.1 = f32[8,1,262144]{2,1,0:T(1,128)} async-done(((f32[8,1,262144]{2,1,0:T(1,128)}), f32[8,1,262144]{2,1,0:T(1,128)}, u32[]{:S(2)}, u32[]{:S(2)}) %all-to-all-start.1) | async-done | bytes 8388640 | tf_op jit(solution)/shard_map/all_to_all | solution.py:73
  188.0 5.0 all-to-all-start
  193.1 0.5 broadcast.193
  193.6 26.6 %reduce = f32[8,262144]{1,0:T(8,128)} reduce(f32[8,1,262144]{2,1,0:T(1,128)} %all-to-all-done.1, f32[]{:T(128)} %broadcast.193), dimensions={1}, to_apply=%all_to_all.52.reduce_sub_computation | reduce | bytes 16777220 | tf_op jit(solution)/shard_map/all_to_all | solution.py:73
  220.2 25.3 %reshape.131 = f32[128,32,16,32]{3,2,1,0:T(8,128)} reshape(f32[8,262144]{1,0:T(8,128)} %reduce) | data formatting | bytes 16777216
  245.5 32.2 %copy.61 = f32[32,32,8,16,16]{1,4,3,2,0:T(8,128)} copy(f32[32,32,8,16,16]{1,3,0,4,2:T(8,128)} %bitcast.96) | data formatting | bytes 16777216 | tf_op jit(solution)/shard_map/all_to_all | solution.py:73
  277.7 22.5 %copy.62 = f32[32,32,128,16]{2,1,3,0:T(8,128)} copy(f32[32,32,128,16]{1,3,2,0:T(8,128)} %bitcast.97) | data formatting | bytes 16777216 | tf_op jit(solution)/shard_map/all_to_all | solution.py:73
  300.2 11.6 %fusion.30 = f32[128,32,32,16]{0,2,3,1:T(8,128)} fusion(f32[32,32,128,16]{2,1,3,0:T(8,128)} %copy.62), kind=kOutput, calls=%fused_computation.55 | convolution fusion | flops 3221454848 | bytes 16777216 | tf_op jit(solution)/shard_map/pxyz,yk->pxkz/dot_general | solution.py:77
  311.8 0.0 all-to-all-done
  311.8 26.4 %reduce.1 = f32[8,262144]{1,0:T(8,128)} reduce(f32[8,1,262144]{2,1,0:T(1,128)} %all-to-all-done, f32[]{:T(128)} %broadcast.193), dimensions={1}, to_apply=%all_to_all.48.reduce_sub_computation | reduce | bytes 16777220 | tf_op jit(solution)/shard_map/all_to_all | solution.py:72
  338.1 25.3 %reshape.133 = f32[128,32,16,32]{3,2,1,0:T(8,128)} reshape(f32[8,262144]{1,0:T(8,128)} %reduce.1) | data formatting | bytes 16777216
  363.4 32.0 %copy.57 = f32[32,32,8,16,16]{1,4,3,2,0:T(8,128)} copy(f32[32,32,8,16,16]{1,3,0,4,2:T(8,128)} %bitcast.98) | data formatting | bytes 16777216 | tf_op jit(solution)/shard_map/all_to_all | solution.py:72
  395.4 22.7 %copy.58 = f32[32,32,128,16]{2,1,3,0:T(8,128)} copy(f32[32,32,128,16]{1,3,2,0:T(8,128)} %bitcast.99) | data formatting | bytes 16777216 | tf_op jit(solution)/shard_map/all_to_all | solution.py:72
  418.1 13.0 %subtract_bitcast_fusion = f32[32,32,128,16]{2,1,3,0:T(8,128)} fusion(f32[128,32,32,16]{0,2,3,1:T(8,128)} %fusion.30, f32[32,32,128,16]{2,1,3,0:T(8,128)} %copy.58), kind=kOutput, calls=%fused_computation.14 | convolution fusion | flops 3223552000 | bytes 25165824 | tf_op jit(solution)/shard_map/pxyz,yk->pxkz/dot_general | solution.py:77
  431.1 26.3 %copy.68 = f32[32,32,128,16]{1,3,0,2:T(8,128)} copy(f32[32,32,128,16]{2,1,3,0:T(8,128)} %subtract_bitcast_fusion) | data formatting | bytes 16777216 | tf_op jit(solution)/shard_map/sub | solution.py:77
  457.5 33.5 %reshape.134 = f32[4,1,524288]{2,1,0:T(1,128)} reshape(f32[128,32,16,32]{3,2,1,0:T(8,128)} %bitcast.94) | data formatting | bytes 16777216
  490.9 6.2 all-to-all-start.3
  497.1 10.2 fusion.32
  507.4 11.8 %add_bitcast_fusion = f32[32,32,128,16]{2,1,3,0:T(8,128)} fusion(f32[128,32,32,16]{0,2,3,1:T(8,128)S(1)} %fusion.32, f32[32,32,128,16]{2,1,3,0:T(8,128)} %copy.62), kind=kOutput, calls=%fused_computation.15 | convolution fusion | flops 3223552000 | bytes 25165824 | tf_op jit(solution)/shard_map/pxyz,yk->pxkz/dot_general | solution.py:74
  519.2 26.3 %copy.63 = f32[32,32,128,16]{1,3,0,2:T(8,128)} copy(f32[32,32,128,16]{2,1,3,0:T(8,128)} %add_bitcast_fusion) | data formatting | bytes 16777216 | tf_op jit(solution)/shard_map/add | solution.py:74
  545.5 33.5 %reshape.136 = f32[4,1,524288]{2,1,0:T(1,128)} reshape(f32[128,32,16,32]{3,2,1,0:T(8,128)} %bitcast.95) | data formatting | bytes 16777216
  579.0 102.7 %all-to-all-done.3 = f32[4,1,524288]{2,1,0:T(1,128)} async-done(((f32[4,1,524288]{2,1,0:T(1,128)}), f32[4,1,524288]{2,1,0:T(1,128)}, u32[]{:S(2)}, u32[]{:S(2)}) %all-to-all-start.3) | async-done | bytes 8388640 | tf_op jit(solution)/shard_map/all_to_all | solution.py:83
  681.7 5.7 all-to-all-start.2
  687.3 0.0 all-reduce.3.cloned.1.call-start
  687.4 0.8 and_select_fusion
  688.2 0.8 compare_and_fusion
  689.0 0.6 fusion.37
  689.6 28.6 %reduce.2 = f32[4,524288]{1,0:T(4,128)} reduce(f32[4,1,524288]{2,1,0:T(1,128)} %all-to-all-done.3, f32[]{:T(128)} %broadcast.193), dimensions={1}, to_apply=%all_to_all.59.reduce_sub_computation | reduce | bytes 16777220 | tf_op jit(solution)/shard_map/all_to_all | solution.py:83
  718.1 31.1 %reshape.135 = f32[128,32,16,32]{3,2,1,0:T(8,128)} reshape(f32[4,524288]{1,0:T(4,128)} %reduce.2) | data formatting | bytes 16777216
  749.2 37.9 %copy.77 = f32[32,32,4,32,16]{1,2,4,3,0:T(4,128)} copy(f32[32,32,4,32,16]{1,4,0,3,2:T(8,128)} %bitcast.100) | data formatting | bytes 16777216 | tf_op jit(solution)/shard_map/all_to_all | solution.py:83
  787.2 25.7 %reshape.83 = f32[32,128,512]{1,2,0:T(8,128)} reshape(f32[32,4,32,32,16]{2,1,4,3,0:T(4,128)} %bitcast.101) | data formatting | bytes 16777216 | tf_op jit(solution)/shard_map/reshape | solution.py:37
  812.8 11.4 copy.70
  824.3 46.4 %all-to-all-done.2 = f32[4,1,524288]{2,1,0:T(1,128)} async-done(((f32[4,1,524288]{2,1,0:T(1,128)}), f32[4,1,524288]{2,1,0:T(1,128)}, u32[]{:S(2)}, u32[]{:S(2)}) %all-to-all-start.2) | async-done | bytes 8388640 | tf_op jit(solution)/shard_map/all_to_all | solution.py:82
  870.7 28.6 %reduce.3 = f32[4,524288]{1,0:T(4,128)} reduce(f32[4,1,524288]{2,1,0:T(1,128)} %all-to-all-done.2, f32[]{:T(128)} %broadcast.193), dimensions={1}, to_apply=%all_to_all.56.reduce_sub_computation | reduce | bytes 16777220 | tf_op jit(solution)/shard_map/all_to_all | solution.py:82
  899.2 31.1 %reshape.137 = f32[128,32,16,32]{3,2,1,0:T(8,128)} reshape(f32[4,524288]{1,0:T(4,128)} %reduce.3) | data formatting | bytes 16777216
  930.3 37.9 %copy.78 = f32[32,32,4,32,16]{1,2,4,3,0:T(4,128)} copy(f32[32,32,4,32,16]{1,4,0,3,2:T(8,128)} %bitcast.102) | data formatting | bytes 16777216 | tf_op jit(solution)/shard_map/all_to_all | solution.py:82
  968.2 25.7 %reshape.82 = f32[32,128,512]{1,2,0:T(8,128)} reshape(f32[32,4,32,32,16]{2,1,4,3,0:T(4,128)} %bitcast.103) | data formatting | bytes 16777216 | tf_op jit(solution)/shard_map/reshape | solution.py:36
  993.9 11.5 copy.65
  1005.4 6.2 gather_fusion.3
  1011.6 6.2 gather_fusion.2
  1017.8 5.9 fusion.7
  1023.7 11.0 all_gather.6
  1034.7 11.4 all_gather.7
  1046.1 0.8 dynamic-slice_select_fusion.1
  1047.0 0.9 dynamic-slice_select_fusion
  1047.8 0.0 all-reduce.3.cloned.1.call-update
  1047.9 0.2 select_reduce_fusion
  1048.1 50.3 %all-reduce.3.cloned.1.call-done = (f32[32,1024]{0,1:T(8,128)}, f32[32,1024]{0,1:T(8,128)}) async-done(((f32[32,1024]{0,1:T(8,128)}, f32[32,1024]{0,1:T(8,128)}), (f32[32,1024]{0,1:T(8,128)}, f32[32,1024]{0,1:T(8,128)})) %all-reduce.3.cloned.1.call-update) | async-done | bytes 262160 | tf_op jit(solution)/shard_map/psum | solution.py:17
  1098.4 8.2 fusion.8
  1106.5 7.3 fusion.12
  1113.9 10.2 fusion.1
  1124.1 10.2 fusion.3
  1134.3 6.2 pad_maximum_fusion
  (18 shorter events, 0.1 us)
Async XLA Ops:
  88.2 99.8 %all-to-all-start.1 = ((f32[8,1,262144]{2,1,0:T(1,128)}), f32[8,1,262144]{2,1,0:T(1,128)}, u32[]{:S(2)}, u32[]{:S(2)}) async-start(f32[8,1,262144]{2,1,0:T(1,128)} %reshape.130), calls=%async_computation.1 | async-start | bytes 16777216 | tf_op jit(solution)/shard_map/all_to_all | solution.py:73
  188.0 123.7 %all-to-all-start = ((f32[8,1,262144]{2,1,0:T(1,128)}), f32[8,1,262144]{2,1,0:T(1,128)}, u32[]{:S(2)}, u32[]{:S(2)}) async-start(f32[8,1,262144]{2,1,0:T(1,128)} %reshape.132), calls=%async_computation | async-start | bytes 16777216 | tf_op jit(solution)/shard_map/all_to_all | solution.py:72
  490.9 190.7 %all-to-all-start.3 = ((f32[4,1,524288]{2,1,0:T(1,128)}), f32[4,1,524288]{2,1,0:T(1,128)}, u32[]{:S(2)}, u32[]{:S(2)}) async-start(f32[4,1,524288]{2,1,0:T(1,128)} %reshape.134), calls=%async_computation.3 | async-start | bytes 16777216 | tf_op jit(solution)/shard_map/all_to_all | solution.py:83
  681.7 189.0 %all-to-all-start.2 = ((f32[4,1,524288]{2,1,0:T(1,128)}), f32[4,1,524288]{2,1,0:T(1,128)}, u32[]{:S(2)}, u32[]{:S(2)}) async-start(f32[4,1,524288]{2,1,0:T(1,128)} %reshape.136), calls=%async_computation.2 | async-start | bytes 16777216 | tf_op jit(solution)/shard_map/all_to_all | solution.py:82
  687.3 411.0 %all-reduce.3.cloned.1.call-start = ((), (), s32[]{:S(2)}) async-start(), calls=%async_computation.4 | async-start | bytes 2097152 | tf_op jit(solution)/shard_map/psum | solution.py:17
  1017.8 30.1 %copy-start.2 = (s32[32]{0:T(128)S(1)}, s32[32]{0:T(128)}, u32[]{:S(2)}) copy-start(s32[32]{0:T(128)} %param.17) | copy-start | bytes 388
  1017.8 30.1 %copy-start.3 = (s32[32]{0:T(128)S(1)}, s32[32]{0:T(128)}, u32[]{:S(2)}) copy-start(s32[32]{0:T(128)} %param.16) | copy-start | bytes 388
  1017.8 30.1 %copy-start.4 = (f32[64]{0:T(128)S(1)}, f32[64]{0:T(128)}, u32[]{:S(2)}) copy-start(f32[64]{0:T(128)} %param.14) | copy-start | bytes 772
  1017.8 30.1 %copy-start.5 = (f32[64]{0:T(128)S(1)}, f32[64]{0:T(128)}, u32[]{:S(2)}) copy-start(f32[64]{0:T(128)} %param.15) | copy-start | bytes 772
  1098.4 8.2 copy-start.1
  1106.5 7.3 copy-start
Sparse Core Ops, SparseCore 0:
  1048.0 50.3 all-reduce.2
where the time goes:
time: 1160 us; the launch traced here: 1150 us
  local copies, waits for them, and re-layouts  619 us (53%)
  waiting for transfers between devices  234 us (20%)
  other arithmetic  128 us (11%)
  matrix products  109 us (9%)
  blocking collectives  22.4 us (2%)
  starting transfers between devices  22.3 us (2%)
  between operations  13.9 us (1%)
    unnamed x20, local copies, waits for them, and re-layouts  221 us
    all_to_all x1, waiting for transfers between devices, on_device(): lax.all_to_all(y_im, 'row', split_axis=2, concat_axis=1, tiled=True)  103 us
    all_to_all x3, local copies, waits for them, and re-layouts, on_device(): lax.all_to_all(z_im, 'col', split_axis=3, concat_axis=2, tiled=True)  55.2 us
    all_to_all x2, local copies, waits for them, and re-layouts, on_device(): lax.all_to_all(z_re, 'col', split_axis=3, concat_axis=2, tiled=True)  54.7 us
    psum x1, waiting for transfers between devices, spread(): return lax.psum(block, axis)  50.3 us
    all_to_all x1, waiting for transfers between devices, on_device(): lax.all_to_all(y_re, 'row', split_axis=2, concat_axis=1, tiled=True)  46.4 us
    all_to_all x1, local copies, waits for them, and re-layouts, on_device(): lax.all_to_all(y_im, 'row', split_axis=2, concat_axis=1, tiled=True)  37.9 us
    all_to_all x1, local copies, waits for them, and re-layouts, on_device(): lax.all_to_all(y_re, 'row', split_axis=2, concat_axis=1, tiled=True)  37.9 us
  transfers between devices with their start and end apart: 5, of which 4 were waited for; matrix products, arithmetic and copies ran while one was open for 35% of the time, Pallas kernels for 0%

commit v1 on v0

v1 whole, which is shorter than its diff:
```python
import functools
import math

import jax
import jax.numpy as jnp
import ml_dtypes
import numpy as np
from jax import lax
from jax.experimental import pallas as pl
from jax.experimental.pallas import tpu as pltpu
from jax.sharding import PartitionSpec as P

F32 = jnp.float32
BF16 = jnp.bfloat16
LANES = 128
ROW_PAD = 72
VMEM_BYTES = 60 * 1024 * 1024
NT = (((1,), (1,)), ((), ()))


def split(value):
    high = value.astype(BF16)
    return high, (value - high.astype(F32)).astype(BF16)


def z_tables(grid):
    half = grid // 2 + 1
    freq = np.arange(half)[:, None] * np.arange(grid)[None, :] % grid
    angle = freq * (2.0 * math.pi / grid)
    scale = 1.0 / math.sqrt(grid**3)
    table = np.zeros((2 * ROW_PAD, grid), np.float32)
    table[:half] = np.cos(angle) * scale
    table[ROW_PAD : ROW_PAD + half] = -np.sin(angle) * scale
    high = table.astype(ml_dtypes.bfloat16)
    low = (table - high.astype(np.float32)).astype(ml_dtypes.bfloat16)
    return jnp.asarray(np.concatenate([high, high], axis=1)), jnp.asarray(low)


def sort_points(gmap, grid):
    count = gmap.shape[0]
    blocks = count // LANES
    kx = gmap // (grid * grid)
    ky = gmap // grid % grid
    kz = gmap % grid
    flip = kz > grid // 2
    fold = jnp.where(flip, grid - kz, kz)
    kx = jnp.where(flip, (grid - kx) % grid, kx)
    ky = jnp.where(flip, (grid - ky) % grid, ky)
    sign = jnp.where(flip, -1.0, 1.0).astype(F32)
    bins = jnp.arange(LANES, dtype=jnp.int32)
    hot = (fold.reshape(blocks, LANES)[:, :, None] == bins).astype(BF16)
    before = (bins[:, None] > bins[None, :]).astype(BF16)
    within = jnp.einsum("ab,jbk->jak", before, hot, preferred_element_type=F32)
    totals = jnp.sum(hot.astype(F32), axis=1).astype(BF16)
    offset = jnp.dot(before[:blocks, :blocks], totals, preferred_element_type=F32)
    start = jnp.sum(jnp.dot(totals, before.T, preferred_element_type=F32), axis=0)
    place = jnp.sum(hot.astype(F32) * (within + offset[:, None, :] + start), axis=2)
    place = place.reshape(-1).astype(jnp.int32)
    major = (place[:, None] // LANES == jnp.arange(blocks, dtype=jnp.int32)).astype(F32)
    minor = (place[:, None] % LANES == bins).astype(BF16)
    values = jnp.stack([kx.astype(F32), ky.astype(F32), fold.astype(F32), sign], axis=1)
    spread = (values[:, :, None] * major[:, None, :]).reshape(count, 4 * blocks).astype(BF16)
    ordered = lax.dot_general(spread, minor, (((0,), (0,)), ((), ())), preferred_element_type=F32)
    return place, ordered


def partial_kernel(
    dims, val_ref, cond_ref, first_ref, last_ref, corner_ref,
    ordered_ref, wide_ref, low_ref, cos_ref, psi_val_ref, psi_cond_ref,
    out_ref, val_buf, cond_buf, z_buf, zz_buf, acc_ref, sems,
):
    pairs, xb, yb, grid, chunks = dims
    rows = xb * yb
    xi_count = 64 // yb
    xo_count = xb // xi_count
    width = xo_count * pairs
    half = grid // 2 + 1

    def copies(p):
        spot = pl.ds(p * rows, rows)
        return (
            pltpu.make_async_copy(psi_val_ref.at[val_ref[p]], val_buf.at[spot], sems.at[0, p]),
            pltpu.make_async_copy(psi_cond_ref.at[cond_ref[p]], cond_buf.at[spot], sems.at[1, p]),
        )

    @pl.loop(0, pairs)
    def _(p):
        for copy in copies(p):
            copy.start()

    @pl.loop(0, pairs)
    def _(p):
        for copy in copies(p):
            copy.wait()

    @pl.loop(0, 64)
    def _(u):
        y, xi = u // xi_count, u % xi_count
        parts = []
        for xo in range(xo_count):
            spot = pl.ds((xo * xi_count + xi) * yb + y, pairs, stride=rows)
            parts.append(val_buf[spot, :] * cond_buf[spot, :])
        rho = jnp.concatenate(parts, axis=0)
        high, low = split(rho)
        both = jnp.concatenate([high, low], axis=1)
        z = lax.dot_general(wide_ref[...], both, NT, preferred_element_type=F32)
        z = z + lax.dot_general(low_ref[...], high, NT, preferred_element_type=F32)
        for t in range(width // LANES):
            lanes = slice(t * LANES, (t + 1) * LANES)
            z_buf[t, pl.ds(u, ROW_PAD, stride=LANES), :] = z[:ROW_PAD, lanes]
            z_buf[t, pl.ds(64 + u, ROW_PAD, stride=LANES), :] = z[ROW_PAD:, lanes]

    @pl.loop(0, half)
    def _(kz):
        for t in range(width // LANES):
            high, low = split(z_buf[t, pl.ds(pl.multiple_of(kz * LANES, LANES), LANES), :])
            lanes = slice(t * LANES, (t + 1) * LANES)
            zz_buf[pl.ds(pl.multiple_of(kz * 256, 256), LANES), lanes] = high
            zz_buf[pl.ds(pl.multiple_of(kz * 256 + LANES, LANES), LANES), lanes] = low

    lane = lax.broadcasted_iota(jnp.int32, (LANES, LANES), 1)
    u_lane = lane % 64
    y_lane, xi_lane = u_lane // xi_count, u_lane % xi_count
    is_im = lane >= 64
    table = jnp.broadcast_to(cos_ref[...], (LANES, LANES))
    quarter = grid // 4

    def cosine(steps):
        return jnp.take_along_axis(table, steps & (grid - 1), axis=1, mode="promise_in_bounds")

    @pl.loop(0, chunks)
    def _(j):
        def column(v):
            row = ordered_ref[pl.ds(v * chunks + j, 1), :]
            return jnp.broadcast_to(row, (LANES, LANES)).T

        kx = column(0).astype(jnp.int32)
        ky = column(1).astype(jnp.int32)
        fold = column(2)
        sign = column(3)
        steps = ky * y_lane + kx * xi_lane
        top = cosine(steps - jnp.where(is_im, quarter, 0))
        bottom = cosine(steps + jnp.where(is_im, 0, quarter))
        high, low = split(jnp.concatenate([top, bottom], axis=0))
        both = jnp.concatenate([high, high], axis=1)
        acc_ref[...] = jnp.zeros_like(acc_ref)

        @pl.loop(first_ref[j], last_ref[j] + 1)
        def _(f):
            base = pl.multiple_of(f * 256, 256)
            result = jnp.dot(both, zz_buf[pl.ds(base, 256), :], preferred_element_type=F32)
            result = result + jnp.dot(low, zz_buf[pl.ds(base, LANES), :], preferred_element_type=F32)
            mine = fold == f.astype(F32)
            for t in range(width // LANES):
                lanes = slice(t * LANES, (t + 1) * LANES)
                for s in range(2):
                    spot = slice(s * LANES, (s + 1) * LANES)
                    acc_ref[spot, lanes] = jnp.where(mine, result[spot, lanes], acc_ref[spot, lanes])

        m_re = jnp.zeros((LANES, LANES), F32)
        m_im = jnp.zeros((LANES, LANES), F32)
        for t in range(width // LANES):
            lanes = slice(t * LANES, (t + 1) * LANES)
            x_lane = corner_ref[0] + (t * LANES + lane) // pairs * xi_count
            steps = kx * x_lane + ky * corner_ref[1]
            cos_p, sin_p = cosine(steps), cosine(steps - quarter)
            a_re, a_im = acc_ref[:LANES, lanes], acc_ref[LANES:, lanes]
            m_re = m_re + a_re * cos_p + a_im * sin_p
            m_im = m_im + a_im * cos_p - a_re * sin_p
        shift = LANES // 2
        while shift >= pairs:
            m_re = m_re + pltpu.roll(m_re, shift, 1)
            m_im = m_im + pltpu.roll(m_im, shift, 1)
            shift //= 2
        m_im = m_im * sign
        spot = pl.ds(pl.multiple_of(j * LANES, LANES), LANES)
        if pairs < LANES:
            group = chunks * 2 * pairs // LANES
            spot = pl.ds(pl.multiple_of(j % group * LANES, LANES), LANES)
            both_parts = jnp.where(lane // pairs % 2 == 0, m_re, m_im)
            out_ref[spot, :] = jnp.where(lane // (2 * pairs) == j // group, both_parts, out_ref[spot, :])
        else:
            out_ref[spot, :LANES] = m_re
            out_ref[spot, LANES:] = m_im


def sum_plan(rows, mesh_rows, mesh_cols):
    col_bits = [("col", b) for b in range(mesh_cols.bit_length() - 1)]
    row_bits = [("row", b) for b in range(mesh_rows.bit_length() - 1)]
    orders = (
        col_bits + row_bits,
        col_bits[:1] + col_bits[:0:-1] + row_bits,
        col_bits[:1] + row_bits + col_bits[1:],
    )
    unit = 8 * mesh_rows * mesh_cols
    units = rows // unit
    first = -(-units * 3 // 8)
    counts = (first, first, units - 2 * first)
    parts, base = [], 0
    for order, count in zip(orders, counts):
        if count:
            parts.append((base, count * unit, count, order))
            base += count * unit
    return parts


def all_sum_kernel(parts, steps, in_ref, out_ref, data, land, send_sems, recv_sems):
    def bit_of(axis, bit):
        return lax.axis_index(axis) // 2**bit % 2

    def partner(axis, bit):
        return {axis: lax.axis_index(axis) + (1 - 2 * bit_of(axis, bit)) * 2**bit}

    barrier = pltpu.get_barrier_semaphore()
    for axis, bit in parts[0][3]:
        pl.semaphore_signal(barrier, inc=1, device_id=partner(axis, bit), device_id_type=pl.DeviceIdType.MESH)
    pl.semaphore_wait(barrier, steps)

    layout = []
    for base, rows, _, order in parts:
        here, size, spots, lands = base, rows, [], base
        for axis, bit in order:
            size //= 2
            side = bit_of(axis, bit)
            keep = pl.multiple_of(here + side * size, 8)
            away = pl.multiple_of(here + (1 - side) * size, 8)
            spots.append((keep, away, size, lands))
            lands += size
            here = keep
        layout.append(spots)

    def copy_of(k, step):
        order = parts[k][3]
        if step < steps:
            keep, away, size, lands = layout[k][step]
            source = (in_ref if step == 0 else data).at[pl.ds(away, size)]
            target = land.at[pl.ds(lands, size)]
            axis, bit = order[step]
        else:
            back = 2 * steps - 1 - step
            keep, away, size, lands = layout[k][back]
            source = target = out_ref.at[pl.ds(keep, size)]
            axis, bit = order[back]
        return pltpu.make_async_remote_copy(
            src_ref=source,
            dst_ref=target,
            send_sem=send_sems.at[k, step],
            recv_sem=recv_sems.at[k, step],
            device_id=partner(axis, bit),
            device_id_type=pl.DeviceIdType.MESH,
        )

    def add(k, step):
        keep, _, size, lands = layout[k][step]
        source = in_ref if step == 0 else data
        target = out_ref if step == steps - 1 else data
        piece = 8 * parts[k][2] * 2 ** min(steps - step - 1, 2)

        @pl.loop(0, size // piece)
        def _(i):
            spot = pl.ds(pl.multiple_of(keep + i * piece, 8), piece)
            target[spot, :] = source[spot, :] + land[pl.ds(pl.multiple_of(lands + i * piece, 8), piece), :]

    for k in range(len(parts)):
        copy_of(k, 0).start()
    for step in range(2 * steps):
        for k in range(len(parts)):
            copy_of(k, step).wait_recv()
            if step < steps:
                add(k, step)
            if step < 2 * steps - 1:
                copy_of(k, step + 1).start()
    for step in range(2 * steps):
        for k in range(len(parts)):
            copy_of(k, step).wait_send()


def all_sum(value, mesh_rows, mesh_cols):
    parts = sum_plan(value.shape[0], mesh_rows, mesh_cols)
    steps = len(parts[0][3])
    vmem_spec = pl.BlockSpec(memory_space=pltpu.VMEM)
    return pl.pallas_call(
        functools.partial(all_sum_kernel, parts, steps),
        out_shape=jax.ShapeDtypeStruct(value.shape, F32),
        in_specs=[vmem_spec],
        out_specs=vmem_spec,
        scratch_shapes=[
            pltpu.VMEM(value.shape, F32),
            pltpu.VMEM(value.shape, F32),
            pltpu.SemaphoreType.DMA((len(parts), 2 * steps)),
            pltpu.SemaphoreType.DMA((len(parts), 2 * steps)),
        ],
        compiler_params=pltpu.CompilerParams(
            collective_id=0, has_side_effects=True, vmem_limit_bytes=VMEM_BYTES
        ),
        name="all_sum",
    )(value)


def update_kernel(dims, row_place, col_place, total_ref, weight_ref, chi_ref, out_ref, m_ref, row_buf, col_buf, right_buf):
    pairs, step_rows, cols, wide = dims
    step = pl.program_id(0)

    def gather(place, base, buf, count):
        @pl.loop(0, count // 8)
        def _(i):
            for k in range(8):
                buf[pl.ds(i * 8 + k, 1), :] = m_ref[pl.ds(place[base + i * 8 + k], 1), :]

    def join(value, right):
        high, low = split(value)
        if 2 * pairs < LANES:
            lane = lax.broadcasted_iota(jnp.int32, value.shape, 1)
            keep = lane < 2 * pairs
            high32, low32 = high.astype(F32), low.astype(F32)
            if right:
                return jnp.concatenate([high, jnp.where(keep, low32, 0.0).astype(BF16)], axis=1)
            return jnp.concatenate(
                [jnp.where(keep, high32, low32).astype(BF16), jnp.where(keep, high32, 0.0).astype(BF16)], axis=1
            )
        return jnp.concatenate([high, high, low] if right else [high, low, high], axis=1)

    @pl.when(step == 0)
    def _():
        packed = total_ref.shape[0]
        piece = 64

        @pl.loop(0, packed // piece)
        def _(i):
            value = total_ref[pl.ds(pl.multiple_of(i * piece, piece), piece), :]
            lane = lax.broadcasted_iota(jnp.int32, value.shape, 1)
            for q in range(m_ref.shape[0] // packed):
                part = value
                if 2 * pairs < wide:
                    part = jnp.where(lane // (2 * pairs) == q, value, 0.0)
                    shift = 2 * pairs
                    while shift < wide:
                        part = part + pltpu.roll(part, shift, 1)
                        shift *= 2
                m_ref[pl.ds(pl.multiple_of(q * packed + i * piece, piece), piece), :] = part

        gather(col_place, 0, col_buf, cols)
        right_buf[...] = join(col_buf[...], True)

    gather(row_place, step * step_rows, row_buf, step_rows)
    left = row_buf[...] * weight_ref[...]
    lane = lax.broadcasted_iota(jnp.int32, left.shape, 1)
    turned = pltpu.roll(left, wide - pairs, 1)
    turned = jnp.where(lane // pairs % 2 == 0, turned, -turned)
    out_ref[0] = chi_ref[0] + lax.dot_general(join(left, False), right_buf[...], NT, preferred_element_type=F32)
    out_ref[1] = chi_ref[1] + lax.dot_general(join(turned, False), right_buf[...], NT, preferred_element_type=F32)


def on_device(psi_val, psi_cond, eps_val, eps_cond, val_index, cond_index, gmap, chi0_in):
    pairs = val_index.shape[0]
    bands_v, xb, yb, grid = psi_val.shape
    bands_c = psi_cond.shape[0]
    points = gmap.shape[0]
    chunks = points // LANES
    row_pos, col_pos = lax.axis_index("row"), lax.axis_index("col")
    place, ordered = sort_points(gmap, grid)
    fold = ordered[2 * chunks : 3 * chunks].astype(jnp.int32)
    corner = jnp.stack([row_pos * xb, col_pos * yb]).astype(jnp.int32)
    z_wide, z_low = z_tables(grid)
    cos_row = jnp.asarray(np.cos(np.arange(grid) * (2.0 * math.pi / grid))[None, :], F32)
    wide = max(LANES, 2 * pairs)
    xi_count = 64 // yb
    width = xb // xi_count * pairs
    rows = xb * yb
    any_spec = pl.BlockSpec(memory_space=pl.ANY)
    vmem_spec = pl.BlockSpec(memory_space=pltpu.VMEM)
    partial = pl.pallas_call(
        functools.partial(partial_kernel, (pairs, xb, yb, grid, chunks)),
        out_shape=jax.ShapeDtypeStruct((points * 2 * pairs // wide, wide), F32),
        grid_spec=pltpu.PrefetchScalarGridSpec(
            num_scalar_prefetch=5,
            grid=(),
            in_specs=[vmem_spec] * 4 + [any_spec] * 2,
            out_specs=vmem_spec,
            scratch_shapes=[
                pltpu.VMEM((pairs * rows, grid), F32),
                pltpu.VMEM((pairs * rows, grid), F32),
                pltpu.VMEM((width // LANES, ROW_PAD * LANES, LANES), F32),
                pltpu.VMEM(((grid // 2 + 1) * 256, width), BF16),
                pltpu.VMEM((256, width), F32),
                pltpu.SemaphoreType.DMA((2, pairs)),
            ],
        ),
        compiler_params=pltpu.CompilerParams(vmem_limit_bytes=VMEM_BYTES),
        name="partial_elements",
    )(
        val_index, cond_index, fold[:, 0], fold[:, LANES - 1], corner,
        ordered, z_wide, z_low, cos_row,
        psi_val.reshape(bands_v, rows, grid), psi_cond.reshape(bands_c, rows, grid),
    )
    total = all_sum(partial, lax.axis_size("row"), lax.axis_size("col"))

    val_hot = val_index[:, None] == jnp.arange(bands_v, dtype=jnp.int32)[None, :]
    cond_hot = cond_index[:, None] == jnp.arange(bands_c, dtype=jnp.int32)[None, :]
    energy_v = jnp.sum(jnp.where(val_hot, eps_val[None, :], 0.0), axis=1)
    energy_c = jnp.sum(jnp.where(cond_hot, eps_cond[None, :], 0.0), axis=1)
    weight = -6.0 / (math.sqrt(pairs) * (energy_c - energy_v))
    weight = jnp.tile(weight, wide // pairs)[None, :]

    _, row_span, col_span = chi0_in.shape
    row_place = lax.dynamic_slice_in_dim(place, row_pos * row_span, row_span, 0)
    col_place = lax.dynamic_slice_in_dim(place, col_pos * col_span, col_span, 0)
    step_rows = 256
    k_width = 256 if 2 * pairs < LANES else 3 * wide
    chi_spec = pl.BlockSpec((2, step_rows, col_span), lambda i, *_: (0, i, 0))
    return pl.pallas_call(
        functools.partial(update_kernel, (pairs, step_rows, col_span, wide)),
        out_shape=jax.ShapeDtypeStruct(chi0_in.shape, F32),
        grid_spec=pltpu.PrefetchScalarGridSpec(
            num_scalar_prefetch=2,
            grid=(row_span // step_rows,),
            in_specs=[vmem_spec, vmem_spec, chi_spec],
            out_specs=chi_spec,
            scratch_shapes=[
                pltpu.VMEM((points, wide), F32),
                pltpu.VMEM((step_rows, wide), F32),
                pltpu.VMEM((col_span, wide), F32),
                pltpu.VMEM((col_span, k_width), BF16),
            ],
        ),
        compiler_params=pltpu.CompilerParams(vmem_limit_bytes=VMEM_BYTES),
        name="chi_update",
    )(row_place, col_place, total, weight, chi0_in)


def solution(mesh):
    return jax.shard_map(
        on_device,
        mesh=mesh,
        in_specs=(
            P(None, "row", "col", None),
            P(None, "row", "col", None),
            P(),
            P(),
            P(),
            P(),
            P(),
            P(None, "row", "col"),
        ),
        out_specs=P(None, "row", "col"),
        check_vma=False,
    )
```

time: 1160 us -> 197 us (0.17); the launches traced: 1150 us -> 197 us
  local copies, waits for them, and re-layouts: 619 us -> 2.58 us
  waiting for transfers between devices: 234 us -> 0 us
  Pallas kernels: 0 us -> 186 us
  other arithmetic: 128 us -> 4.83 us
  matrix products: 109 us -> 3.6 us
  blocking collectives: 22.4 us -> 0 us
  starting transfers between devices: 22.3 us -> 0 us
  between operations: 13.9 us -> 0.11 us
    unnamed x20 -> x2, local copies, waits for them, and re-layouts: 221 us -> 0.01 us
    pallas_call x0 -> x3, Pallas kernels: none -> 186 us  [the longest x1 116 us: on_device(): pl.pallas_call(functools.partial(partial_kernel, (pairs, xb, yb, grid, ch...]
    all_to_all x7 -> x0, local copies, waits for them, and re-layouts: 186 us -> none  [the longest x3 55.2 us: on_device(): lax.all_to_all(z_im, 'col', split_axis=3, concat_axis=2, tiled=True)]
    all_to_all x4 -> x0, waiting for transfers between devices: 184 us -> none  [the longest x1 103 us: on_device(): lax.all_to_all(y_im, 'row', split_axis=2, concat_axis=1, tiled=True)]
    all_to_all x4 -> x0, other arithmetic: 110 us -> none  [the longest x1 28.6 us: on_device(): lax.all_to_all(y_im, 'row', split_axis=2, concat_axis=1, tiled=True)]
    dot_general x10 -> x4, matrix products: 109 us -> 3.6 us  [the longest x1 1.89 us: sort_points(): within = jnp.einsum('ab,jbk->jak', before, hot, preferred_element_type=F32)]
    reshape x4 -> x0, local copies, waits for them, and re-layouts: 74.2 us -> none  [the longest x2 37.1 us: pick_points(): flat_re = real_part.reshape(count, real_part.shape[1], -1)]
    psum x1 -> x0, waiting for transfers between devices: 50.3 us -> none  [spread(): return lax.psum(block, axis)]
  transfers between devices with their start and end apart: 5 -> 0, of which waited for: 4 -> 0; matrix products, arithmetic and copies ran while one was open for 35% -> 0% of each run, Pallas kernels for 0% -> 0%
where the time goes in v1:
time: 197 us
  Pallas kernels  186 us (94%)
  other arithmetic  4.83 us (2%)
  matrix products  3.6 us (2%)
  local copies, waits for them, and re-layouts  2.58 us (1%)
    pallas_call x1, Pallas kernels, on_device(): pl.pallas_call(functools.partial(partial_kernel, (pairs, xb, yb, grid, ch...  116 us
    pallas_call x1, Pallas kernels, all_sum(): pl.pallas_call(functools.partial(all_sum_kernel, parts, steps), out_shape...  44.3 us
    pallas_call x1, Pallas kernels, on_device(): pl.pallas_call(functools.partial(update_kernel, (pairs, step_rows, col_sp...  25.2 us

profile of v1, /device:TPU:0, one launch (start us, length us, event | category | flops | bytes accessed | tf_op | source)
XLA Modules:
  0.0 197.0 jit_solution(15662003226754536272)
XLA Ops:
  0.0 0.6 pad_add_fusion.corner_ref
  0.6 0.9 select_reduce_fusion
  1.5 0.6 broadcast_in_dim_tile.3.weight_ref
  2.1 0.8 broadcast_select_fusion
  2.9 0.9 fusion.12
  3.8 0.1 pad_maximum_fusion
  3.9 0.7 fusion.4
  4.6 0.2 convolution_reduce_fusion
  4.8 0.1 fusion.19
  4.9 1.9 fusion
  6.8 0.6 dynamic_slice.7.col_place
  7.4 0.6 dynamic_slice.6.row_place
  8.1 0.2 fusion.7
  8.2 0.7 multiply_convert_fusion
  8.9 1.4 fusion.3.ordered_ref
  10.3 0.0 copy-start
  10.3 0.8 slice_reduce_fusion
  11.1 0.0 copy-done
  11.1 116.5 %partial_elements.1.in_ref = f32[4096,128]{1,0:T(8,128)} custom-call(s32[32]{0:T(128)} %val_ref.1, s32[32]{0:T(128)} %cond_ref.1, s32[64]{0:T(128)} %get-tuple-element.6.first_ref, s32[64]{0:T(128)} %get-tuple-element.5.last_ref, s32[2]{0:T(128)} %pad_add_fusion.corner_ref, f32[256,128]{1,0:T(8,128)} %copy-done, bf16[144,256]{1,0:T(8,128)(2,1)} %constant.111.clone.wide_ref, ...), custom_call_target="tpu_custom_call" | custom-call | tf_op jit(solution)/shard_map/partial_elements/pallas_call | solution.py:372
  127.6 44.3 %all_sum.1.total_ref = f32[4096,128]{1,0:T(8,128)} custom-call(f32[4096,128]{1,0:T(8,128)} %partial_elements.1.in_ref), custom_call_target="tpu_custom_call" | custom-call | tf_op jit(solution)/shard_map/all_sum/pallas_call | solution.py:282
  171.9 25.2 %chi_update.1 = f32[2,2048,1024]{2,1,0:T(8,128)} custom-call(s32[2048]{0:T(1024)} %dynamic_slice.6.row_place, s32[1024]{0:T(1024)} %dynamic_slice.7.col_place, f32[4096,128]{1,0:T(8,128)} %all_sum.1.total_ref, f32[1,128]{1,0:T(1,128)} %broadcast_in_dim_tile.3.weight_ref, f32[2,2048,1024]{2,1,0:T(8,128)} %chi_ref.1), custom_call_target="tpu_custom_call" | custom-call | tf_op jit(solution)/shard_map/chi_update/pallas_call | solution.py:411
  (6 shorter events, 0.1 us)
Async XLA Ops:
  10.3 0.8 copy-start

commit v2 on v1

--- a/solution.py
+++ b/solution.py
@@ -33,7 +33,8 @@
     table[ROW_PAD : ROW_PAD + half] = -np.sin(angle) * scale
     high = table.astype(ml_dtypes.bfloat16)
     low = (table - high.astype(np.float32)).astype(ml_dtypes.bfloat16)
-    return jnp.asarray(np.concatenate([high, high], axis=1)), jnp.asarray(low)
+    top = np.concatenate([high, high], axis=1)
+    return jnp.asarray(np.concatenate([top, np.concatenate([low, np.zeros_like(low)], axis=1)], axis=0))
 
 
 def sort_points(gmap, grid):
@@ -66,8 +67,8 @@
 
 def partial_kernel(
     dims, val_ref, cond_ref, first_ref, last_ref, corner_ref,
-    ordered_ref, wide_ref, low_ref, cos_ref, psi_val_ref, psi_cond_ref,
-    out_ref, val_buf, cond_buf, z_buf, zz_buf, acc_ref, sems,
+    ordered_ref, wide_ref, cos_ref, psi_val_ref, psi_cond_ref,
+    out_ref, val_buf, cond_buf, z_buf, zz_buf, sems,
 ):
     pairs, xb, yb, grid, chunks = dims
     rows = xb * yb
@@ -93,22 +94,25 @@
         for copy in copies(p):
             copy.wait()
 
-    @pl.loop(0, 64)
-    def _(u):
+    def transform(u):
         y, xi = u // xi_count, u % xi_count
         parts = []
         for xo in range(xo_count):
             spot = pl.ds((xo * xi_count + xi) * yb + y, pairs, stride=rows)
             parts.append(val_buf[spot, :] * cond_buf[spot, :])
-        rho = jnp.concatenate(parts, axis=0)
-        high, low = split(rho)
+        high, low = split(jnp.concatenate(parts, axis=0))
         both = jnp.concatenate([high, low], axis=1)
         z = lax.dot_general(wide_ref[...], both, NT, preferred_element_type=F32)
-        z = z + lax.dot_general(low_ref[...], high, NT, preferred_element_type=F32)
-        for t in range(width // LANES):
-            lanes = slice(t * LANES, (t + 1) * LANES)
-            z_buf[t, pl.ds(u, ROW_PAD, stride=LANES), :] = z[:ROW_PAD, lanes]
-            z_buf[t, pl.ds(64 + u, ROW_PAD, stride=LANES), :] = z[ROW_PAD:, lanes]
+        return z[: 2 * ROW_PAD] + z[2 * ROW_PAD :]
+
+    @pl.loop(0, 16)
+    def _(i):
+        results = [transform(i * 4 + k) for k in range(4)]
+        for k, z in enumerate(results):
+            for t in range(width // LANES):
+                lanes = slice(t * LANES, (t + 1) * LANES)
+                z_buf[t, pl.ds(i * 4 + k, ROW_PAD, stride=LANES), :] = z[:ROW_PAD, lanes]
+                z_buf[t, pl.ds(64 + i * 4 + k, ROW_PAD, stride=LANES), :] = z[ROW_PAD:, lanes]
 
     @pl.loop(0, half)
     def _(kz):
@@ -128,8 +132,7 @@
     def cosine(steps):
         return jnp.take_along_axis(table, steps & (grid - 1), axis=1, mode="promise_in_bounds")
 
-    @pl.loop(0, chunks)
-    def _(j):
+    def elements(j, bins):
         def column(v):
             row = ordered_ref[pl.ds(v * chunks + j, 1), :]
             return jnp.broadcast_to(row, (LANES, LANES)).T
@@ -141,22 +144,16 @@
         steps = ky * y_lane + kx * xi_lane
         top = cosine(steps - jnp.where(is_im, quarter, 0))
         bottom = cosine(steps + jnp.where(is_im, 0, quarter))
-        high, low = split(jnp.concatenate([top, bottom], axis=0))
-        both = jnp.concatenate([high, high], axis=1)
-        acc_ref[...] = jnp.zeros_like(acc_ref)
-
-        @pl.loop(first_ref[j], last_ref[j] + 1)
-        def _(f):
-            base = pl.multiple_of(f * 256, 256)
-            result = jnp.dot(both, zz_buf[pl.ds(base, 256), :], preferred_element_type=F32)
-            result = result + jnp.dot(low, zz_buf[pl.ds(base, LANES), :], preferred_element_type=F32)
+        left, right = [], []
+        for f in bins:
             mine = fold == f.astype(F32)
-            for t in range(width // LANES):
-                lanes = slice(t * LANES, (t + 1) * LANES)
-                for s in range(2):
-                    spot = slice(s * LANES, (s + 1) * LANES)
-                    acc_ref[spot, lanes] = jnp.where(mine, result[spot, lanes], acc_ref[spot, lanes])
-
+            high, low = split(jnp.concatenate([jnp.where(mine, top, 0.0), jnp.where(mine, bottom, 0.0)], axis=0))
+            base = pl.multiple_of(jnp.minimum(f, half - 1) * 256, 256)
+            left += [high, high, low]
+            right += [zz_buf[pl.ds(base, 256), :], zz_buf[pl.ds(base, LANES), :]]
+        result = jnp.dot(
+            jnp.concatenate(left, axis=1), jnp.concatenate(right, axis=0), preferred_element_type=F32
+        )
         m_re = jnp.zeros((LANES, LANES), F32)
         m_im = jnp.zeros((LANES, LANES), F32)
         for t in range(width // LANES):
@@ -164,7 +161,7 @@
             x_lane = corner_ref[0] + (t * LANES + lane) // pairs * xi_count
             steps = kx * x_lane + ky * corner_ref[1]
             cos_p, sin_p = cosine(steps), cosine(steps - quarter)
-            a_re, a_im = acc_ref[:LANES, lanes], acc_ref[LANES:, lanes]
+            a_re, a_im = result[:LANES, lanes], result[LANES:, lanes]
             m_re = m_re + a_re * cos_p + a_im * sin_p
             m_im = m_im + a_im * cos_p - a_re * sin_p
         shift = LANES // 2
@@ -173,15 +170,38 @@
             m_im = m_im + pltpu.roll(m_im, shift, 1)
             shift //= 2
         m_im = m_im * sign
-        spot = pl.ds(pl.multiple_of(j * LANES, LANES), LANES)
         if pairs < LANES:
-            group = chunks * 2 * pairs // LANES
+            return (jnp.where(lane // pairs % 2 == 0, m_re, m_im),)
+        return m_re, m_im
+
+    packs = max(1, LANES // (2 * pairs))
+    group = chunks // packs
+    together = packs if packs > 1 else 2
+
+    @pl.loop(0, chunks // together)
+    def _(i):
+        numbers = [i + k * (chunks // together) for k in range(together)]
+        found = [elements(j, (first_ref[j], first_ref[j] + 1)) for j in numbers]
+        if packs > 1:
+            value = found[0][0]
+            for k in range(1, packs):
+                value = jnp.where(lane // (2 * pairs) == k, found[k][0], value)
+            out_ref[pl.ds(pl.multiple_of(i * LANES, LANES), LANES), :] = value
+        else:
+            for j, pieces in zip(numbers, found):
+                for t, piece in enumerate(pieces):
+                    out_ref[pl.ds(pl.multiple_of(j * LANES, LANES), LANES), t * LANES : (t + 1) * LANES] = piece
+
+    @pl.loop(0, chunks)
+    def _(j):
+        @pl.loop(first_ref[j] + 2, last_ref[j] + 1)
+        def _(f):
             spot = pl.ds(pl.multiple_of(j % group * LANES, LANES), LANES)
-            both_parts = jnp.where(lane // pairs % 2 == 0, m_re, m_im)
-            out_ref[spot, :] = jnp.where(lane // (2 * pairs) == j // group, both_parts, out_ref[spot, :])
-        else:
-            out_ref[spot, :LANES] = m_re
-            out_ref[spot, LANES:] = m_im
+            for t, piece in enumerate(elements(j, (f,))):
+                if packs > 1:
+                    piece = jnp.where(lane // (2 * pairs) == j // group, piece, 0.0)
+                lanes = slice(t * LANES, (t + 1) * LANES)
+                out_ref[spot, lanes] = out_ref[spot, lanes] + piece
 
 
 def sum_plan(rows, mesh_rows, mesh_cols):
@@ -302,23 +322,30 @@
     step = pl.program_id(0)
 
     def gather(place, base, buf, count):
-        @pl.loop(0, count // 8)
+        @pl.loop(0, count // 16)
         def _(i):
-            for k in range(8):
-                buf[pl.ds(i * 8 + k, 1), :] = m_ref[pl.ds(place[base + i * 8 + k], 1), :]
-
-    def join(value, right):
+            found = [m_ref[pl.ds(place[base + i * 16 + k], 1), :] for k in range(16)]
+            for half in range(2):
+                spot = pl.ds(pl.multiple_of(i * 16 + half * 8, 8), 8)
+                buf[spot, :] = jnp.concatenate(found[half * 8 : half * 8 + 8], axis=0)
+
+    def join(value):
         high, low = split(value)
         if 2 * pairs < LANES:
             lane = lax.broadcasted_iota(jnp.int32, value.shape, 1)
             keep = lane < 2 * pairs
             high32, low32 = high.astype(F32), low.astype(F32)
-            if right:
-                return jnp.concatenate([high, jnp.where(keep, low32, 0.0).astype(BF16)], axis=1)
             return jnp.concatenate(
                 [jnp.where(keep, high32, low32).astype(BF16), jnp.where(keep, high32, 0.0).astype(BF16)], axis=1
             )
-        return jnp.concatenate([high, high, low] if right else [high, low, high], axis=1)
+        return jnp.concatenate([high, low, high], axis=1)
+
+    def join_right(value):
+        high, low = split(value)
+        if 2 * pairs < LANES:
+            keep = lax.broadcasted_iota(jnp.int32, value.shape, 0) < 2 * pairs
+            return jnp.concatenate([high, jnp.where(keep, low.astype(F32), 0.0).astype(BF16)], axis=0)
+        return jnp.concatenate([high, high, low], axis=0)
 
     @pl.when(step == 0)
     def _():
@@ -340,15 +367,15 @@
                 m_ref[pl.ds(pl.multiple_of(q * packed + i * piece, piece), piece), :] = part
 
         gather(col_place, 0, col_buf, cols)
-        right_buf[...] = join(col_buf[...], True)
+        right_buf[...] = join_right(col_buf[...].T)
 
     gather(row_place, step * step_rows, row_buf, step_rows)
     left = row_buf[...] * weight_ref[...]
     lane = lax.broadcasted_iota(jnp.int32, left.shape, 1)
     turned = pltpu.roll(left, wide - pairs, 1)
     turned = jnp.where(lane // pairs % 2 == 0, turned, -turned)
-    out_ref[0] = chi_ref[0] + lax.dot_general(join(left, False), right_buf[...], NT, preferred_element_type=F32)
-    out_ref[1] = chi_ref[1] + lax.dot_general(join(turned, False), right_buf[...], NT, preferred_element_type=F32)
+    out_ref[0] = chi_ref[0] + jnp.dot(join(left), right_buf[...], preferred_element_type=F32)
+    out_ref[1] = chi_ref[1] + jnp.dot(join(turned), right_buf[...], preferred_element_type=F32)
 
 
 def on_device(psi_val, psi_cond, eps_val, eps_cond, val_index, cond_index, gmap, chi0_in):
@@ -361,7 +388,7 @@
     place, ordered = sort_points(gmap, grid)
     fold = ordered[2 * chunks : 3 * chunks].astype(jnp.int32)
     corner = jnp.stack([row_pos * xb, col_pos * yb]).astype(jnp.int32)
-    z_wide, z_low = z_tables(grid)
+    z_wide = z_tables(grid)
     cos_row = jnp.asarray(np.cos(np.arange(grid) * (2.0 * math.pi / grid))[None, :], F32)
     wide = max(LANES, 2 * pairs)
     xi_count = 64 // yb
@@ -375,14 +402,13 @@
         grid_spec=pltpu.PrefetchScalarGridSpec(
             num_scalar_prefetch=5,
             grid=(),
-            in_specs=[vmem_spec] * 4 + [any_spec] * 2,
+            in_specs=[vmem_spec] * 3 + [any_spec] * 2,
             out_specs=vmem_spec,
             scratch_shapes=[
                 pltpu.VMEM((pairs * rows, grid), F32),
                 pltpu.VMEM((pairs * rows, grid), F32),
                 pltpu.VMEM((width // LANES, ROW_PAD * LANES, LANES), F32),
                 pltpu.VMEM(((grid // 2 + 1) * 256, width), BF16),
-                pltpu.VMEM((256, width), F32),
                 pltpu.SemaphoreType.DMA((2, pairs)),
             ],
         ),
@@ -390,7 +416,7 @@
         name="partial_elements",
     )(
         val_index, cond_index, fold[:, 0], fold[:, LANES - 1], corner,
-        ordered, z_wide, z_low, cos_row,
+        ordered, z_wide, cos_row,
         psi_val.reshape(bands_v, rows, grid), psi_cond.reshape(bands_c, rows, grid),
     )
     total = all_sum(partial, lax.axis_size("row"), lax.axis_size("col"))
@@ -420,7 +446,7 @@
                 pltpu.VMEM((points, wide), F32),
                 pltpu.VMEM((step_rows, wide), F32),
                 pltpu.VMEM((col_span, wide), F32),
-                pltpu.VMEM((col_span, k_width), BF16),
+                pltpu.VMEM((k_width, col_span), BF16),
             ],
         ),
         compiler_params=pltpu.CompilerParams(vmem_limit_bytes=VMEM_BYTES),

time: 197 us -> 151 us (0.77)
  Pallas kernels: 186 us -> 139 us
    pallas_call x1, Pallas kernels: 116 us -> 70.2 us  [on_device(): pl.pallas_call(functools.partial(partial_kernel, (pairs, xb, yb, grid, ch...]
where the time goes in v2:
time: 151 us; the launch traced here: 150 us
  Pallas kernels  139 us (92%)
  other arithmetic  4.83 us (3%)
  matrix products  3.6 us (2%)
  local copies, waits for them, and re-layouts  2.58 us (2%)
    pallas_call x1, Pallas kernels, on_device(): pl.pallas_call(functools.partial(partial_kernel, (pairs, xb, yb, grid, ch...  70.2 us
    pallas_call x1, Pallas kernels, all_sum(): pl.pallas_call(functools.partial(all_sum_kernel, parts, steps), out_shape...  44.3 us
    pallas_call x1, Pallas kernels, on_device(): pl.pallas_call(functools.partial(update_kernel, (pairs, step_rows, col_sp...  24.6 us

profile of v2, /device:TPU:0, one launch (start us, length us, event | category | flops | bytes accessed | tf_op | source)
XLA Modules:
  0.0 150.2 jit_solution(11214566447663492315)
XLA Ops:
  0.0 0.6 pad_add_fusion.corner_ref
  0.6 0.9 select_reduce_fusion
  1.5 0.6 broadcast_in_dim_tile.3.weight_ref
  2.1 0.8 broadcast_select_fusion
  2.9 0.9 fusion.12
  3.8 0.1 pad_maximum_fusion
  3.9 0.7 fusion.4
  4.6 0.2 convolution_reduce_fusion
  4.8 0.1 fusion.19
  4.9 1.9 %fusion = f32[64,128]{1,0:T(8,128)S(1)} fusion(f32[128]{0:T(128)S(1)} %convolution_reduce_fusion, f32[64,128]{1,0:T(8,128)S(1)} %fusion.19, s32[64,128]{1,0:T(8,128)S(1)} %get-tuple-element.10), kind=kOutput, calls=%fused_computation.2 | convolution fusion | flops 276832256 | bytes 98816 | tf_op jit(solution)/shard_map/ab,jbk->jak/dot_general | solution.py:54
  6.8 0.6 dynamic_slice.7.col_place
  7.4 0.6 dynamic_slice.6.row_place
  8.1 0.2 fusion.7
  8.2 0.7 multiply_convert_fusion
  8.9 1.4 fusion.3.ordered_ref
  10.3 0.0 copy-start
  10.3 0.8 slice_reduce_fusion
  11.1 0.0 copy-done
  11.1 70.2 %partial_elements.1.in_ref = f32[4096,128]{1,0:T(8,128)} custom-call(s32[32]{0:T(128)} %val_ref.1, s32[32]{0:T(128)} %cond_ref.1, s32[64]{0:T(128)} %get-tuple-element.6.first_ref, s32[64]{0:T(128)} %get-tuple-element.5.last_ref, s32[2]{0:T(128)} %pad_add_fusion.corner_ref, f32[256,128]{1,0:T(8,128)} %copy-done, bf16[288,256]{1,0:T(8,128)(2,1)} %constant.109.clone.wide_ref, ...), custom_call_target="tpu_custom_call" | custom-call | tf_op jit(solution)/shard_map/partial_elements/pallas_call | solution.py:399
  81.3 44.3 %all_sum.1.total_ref = f32[4096,128]{1,0:T(8,128)} custom-call(f32[4096,128]{1,0:T(8,128)} %partial_elements.1.in_ref), custom_call_target="tpu_custom_call" | custom-call | tf_op jit(solution)/shard_map/all_sum/pallas_call | solution.py:302
  125.6 24.6 %chi_update.1 = f32[2,2048,1024]{2,1,0:T(8,128)} custom-call(s32[2048]{0:T(1024)} %dynamic_slice.6.row_place, s32[1024]{0:T(1024)} %dynamic_slice.7.col_place, f32[4096,128]{1,0:T(8,128)} %all_sum.1.total_ref, f32[1,128]{1,0:T(1,128)} %broadcast_in_dim_tile.3.weight_ref, f32[2,2048,1024]{2,1,0:T(8,128)} %chi_ref.1), custom_call_target="tpu_custom_call" | custom-call | tf_op jit(solution)/shard_map/chi_update/pallas_call | solution.py:437
  (6 shorter events, 0.1 us)
Async XLA Ops:
  10.3 0.8 copy-start

commit v3 on v2

--- a/solution.py
+++ b/solution.py
@@ -14,6 +14,7 @@
 BF16 = jnp.bfloat16
 LANES = 128
 ROW_PAD = 72
+Z_STRIDE = LANES + 8
 VMEM_BYTES = 60 * 1024 * 1024
 NT = (((1,), (1,)), ((), ()))
 
@@ -78,7 +79,7 @@
     half = grid // 2 + 1
 
     def copies(p):
-        spot = pl.ds(p * rows, rows)
+        spot = pl.ds(pl.multiple_of(p * (rows + 8), 8), rows)
         return (
             pltpu.make_async_copy(psi_val_ref.at[val_ref[p]], val_buf.at[spot], sems.at[0, p]),
             pltpu.make_async_copy(psi_cond_ref.at[cond_ref[p]], cond_buf.at[spot], sems.at[1, p]),
@@ -98,7 +99,7 @@
         y, xi = u // xi_count, u % xi_count
         parts = []
         for xo in range(xo_count):
-            spot = pl.ds((xo * xi_count + xi) * yb + y, pairs, stride=rows)
+            spot = pl.ds((xo * xi_count + xi) * yb + y, pairs, stride=rows + 8)
             parts.append(val_buf[spot, :] * cond_buf[spot, :])
         high, low = split(jnp.concatenate(parts, axis=0))
         both = jnp.concatenate([high, low], axis=1)
@@ -111,13 +112,13 @@
         for k, z in enumerate(results):
             for t in range(width // LANES):
                 lanes = slice(t * LANES, (t + 1) * LANES)
-                z_buf[t, pl.ds(i * 4 + k, ROW_PAD, stride=LANES), :] = z[:ROW_PAD, lanes]
-                z_buf[t, pl.ds(64 + i * 4 + k, ROW_PAD, stride=LANES), :] = z[ROW_PAD:, lanes]
+                z_buf[t, pl.ds(i * 4 + k, ROW_PAD, stride=Z_STRIDE), :] = z[:ROW_PAD, lanes]
+                z_buf[t, pl.ds(64 + i * 4 + k, ROW_PAD, stride=Z_STRIDE), :] = z[ROW_PAD:, lanes]
 
     @pl.loop(0, half)
     def _(kz):
         for t in range(width // LANES):
-            high, low = split(z_buf[t, pl.ds(pl.multiple_of(kz * LANES, LANES), LANES), :])
+            high, low = split(z_buf[t, pl.ds(pl.multiple_of(kz * Z_STRIDE, 8), LANES), :])
             lanes = slice(t * LANES, (t + 1) * LANES)
             zz_buf[pl.ds(pl.multiple_of(kz * 256, 256), LANES), lanes] = high
             zz_buf[pl.ds(pl.multiple_of(kz * 256 + LANES, LANES), LANES), lanes] = low
@@ -176,21 +177,19 @@
 
     packs = max(1, LANES // (2 * pairs))
     group = chunks // packs
-    together = packs if packs > 1 else 2
-
-    @pl.loop(0, chunks // together)
+
+    @pl.loop(0, group // 2)
     def _(i):
-        numbers = [i + k * (chunks // together) for k in range(together)]
-        found = [elements(j, (first_ref[j], first_ref[j] + 1)) for j in numbers]
-        if packs > 1:
-            value = found[0][0]
+        bases = [i, i + group // 2]
+        found = [[elements(b + k * group, (first_ref[b + k * group], first_ref[b + k * group] + 1))
+                  for k in range(packs)] for b in bases]
+        for b, pieces in zip(bases, found):
+            spot = pl.ds(pl.multiple_of(b * LANES, LANES), LANES)
+            value = list(pieces[0])
             for k in range(1, packs):
-                value = jnp.where(lane // (2 * pairs) == k, found[k][0], value)
-            out_ref[pl.ds(pl.multiple_of(i * LANES, LANES), LANES), :] = value
-        else:
-            for j, pieces in zip(numbers, found):
-                for t, piece in enumerate(pieces):
-                    out_ref[pl.ds(pl.multiple_of(j * LANES, LANES), LANES), t * LANES : (t + 1) * LANES] = piece
+                value[0] = jnp.where(lane // (2 * pairs) == k, pieces[k][0], value[0])
+            for t, piece in enumerate(value):
+                out_ref[spot, t * LANES : (t + 1) * LANES] = piece
 
     @pl.loop(0, chunks)
     def _(j):
@@ -217,7 +216,8 @@
     first = -(-units * 3 // 8)
     counts = (first, first, units - 2 * first)
     parts, base = [], 0
-    for order, count in zip(orders, counts):
+    halves = [(o, c - c // 2) for o, c in zip(orders, counts)] + [(o, c // 2) for o, c in zip(orders, counts)]
+    for order, count in halves:
         if count:
             parts.append((base, count * unit, count, order))
             base += count * unit
@@ -317,9 +317,24 @@
     )(value)
 
 
-def update_kernel(dims, row_place, col_place, total_ref, weight_ref, chi_ref, out_ref, m_ref, row_buf, col_buf, right_buf):
+def update_kernel(
+    dims, row_place, col_place, total_ref, weight_ref, chi_ref, out_ref,
+    m_ref, row_buf, col_buf, right_buf, chi_buf, sems,
+):
     pairs, step_rows, cols, wide = dims
-    step = pl.program_id(0)
+    steps = chi_ref.shape[1] // step_rows
+
+    def arrival(step):
+        spot = pl.ds(pl.multiple_of(step * step_rows, step_rows), step_rows)
+        return pltpu.make_async_copy(chi_ref.at[:, spot], chi_buf.at[:, spot], sems.at[0, step])
+
+    def departure(step):
+        spot = pl.ds(pl.multiple_of(step * step_rows, step_rows), step_rows)
+        return pltpu.make_async_copy(chi_buf.at[:, spot], out_ref.at[:, spot], sems.at[1, step])
+
+    @pl.loop(0, steps)
+    def _(step):
+        arrival(step).start()
 
     def gather(place, base, buf, count):
         @pl.loop(0, count // 16)
@@ -347,35 +362,43 @@
             return jnp.concatenate([high, jnp.where(keep, low.astype(F32), 0.0).astype(BF16)], axis=0)
         return jnp.concatenate([high, high, low], axis=0)
 
-    @pl.when(step == 0)
-    def _():
-        packed = total_ref.shape[0]
-        piece = 64
-
-        @pl.loop(0, packed // piece)
-        def _(i):
-            value = total_ref[pl.ds(pl.multiple_of(i * piece, piece), piece), :]
-            lane = lax.broadcasted_iota(jnp.int32, value.shape, 1)
-            for q in range(m_ref.shape[0] // packed):
-                part = value
-                if 2 * pairs < wide:
-                    part = jnp.where(lane // (2 * pairs) == q, value, 0.0)
-                    shift = 2 * pairs
-                    while shift < wide:
-                        part = part + pltpu.roll(part, shift, 1)
-                        shift *= 2
-                m_ref[pl.ds(pl.multiple_of(q * packed + i * piece, piece), piece), :] = part
-
-        gather(col_place, 0, col_buf, cols)
-        right_buf[...] = join_right(col_buf[...].T)
-
-    gather(row_place, step * step_rows, row_buf, step_rows)
-    left = row_buf[...] * weight_ref[...]
-    lane = lax.broadcasted_iota(jnp.int32, left.shape, 1)
-    turned = pltpu.roll(left, wide - pairs, 1)
-    turned = jnp.where(lane // pairs % 2 == 0, turned, -turned)
-    out_ref[0] = chi_ref[0] + jnp.dot(join(left), right_buf[...], preferred_element_type=F32)
-    out_ref[1] = chi_ref[1] + jnp.dot(join(turned), right_buf[...], preferred_element_type=F32)
+    packed = total_ref.shape[0]
+    piece = 64
+
+    @pl.loop(0, packed // piece)
+    def _(i):
+        value = total_ref[pl.ds(pl.multiple_of(i * piece, piece), piece), :]
+        lane = lax.broadcasted_iota(jnp.int32, value.shape, 1)
+        for q in range(m_ref.shape[0] // packed):
+            part = value
+            if 2 * pairs < wide:
+                part = jnp.where(lane // (2 * pairs) == q, value, 0.0)
+                shift = 2 * pairs
+                while shift < wide:
+                    part = part + pltpu.roll(part, shift, 1)
+                    shift *= 2
+            m_ref[pl.ds(pl.multiple_of(q * packed + i * piece, piece), piece), :] = part
+
+    gather(col_place, 0, col_buf, cols)
+    right_buf[...] = join_right(col_buf[...].T)
+
+    @pl.loop(0, steps)
+    def _(step):
+        gather(row_place, step * step_rows, row_buf, step_rows)
+        left = row_buf[...] * weight_ref[...]
+        lane = lax.broadcasted_iota(jnp.int32, left.shape, 1)
+        turned = pltpu.roll(left, wide - pairs, 1)
+        turned = jnp.where(lane // pairs % 2 == 0, turned, -turned)
+        arrival(step).wait()
+        spot = pl.ds(pl.multiple_of(step * step_rows, step_rows), step_rows)
+        for part, factor in enumerate((left, turned)):
+            change = jnp.dot(join(factor), right_buf[...], preferred_element_type=F32)
+            chi_buf[part, spot, :] = chi_buf[part, spot, :] + change
+        departure(step).start()
+
+    @pl.loop(0, steps)
+    def _(step):
+        departure(step).wait()
 
 
 def on_device(psi_val, psi_cond, eps_val, eps_cond, val_index, cond_index, gmap, chi0_in):
@@ -405,9 +428,9 @@
             in_specs=[vmem_spec] * 3 + [any_spec] * 2,
             out_specs=vmem_spec,
             scratch_shapes=[
-                pltpu.VMEM((pairs * rows, grid), F32),
-                pltpu.VMEM((pairs * rows, grid), F32),
-                pltpu.VMEM((width // LANES, ROW_PAD * LANES, LANES), F32),
+                pltpu.VMEM((pairs * (rows + 8), grid), F32),
+                pltpu.VMEM((pairs * (rows + 8), grid), F32),
+                pltpu.VMEM((width // LANES, ROW_PAD * Z_STRIDE, LANES), F32),
                 pltpu.VMEM(((grid // 2 + 1) * 256, width), BF16),
                 pltpu.SemaphoreType.DMA((2, pairs)),
             ],
@@ -433,20 +456,21 @@
     col_place = lax.dynamic_slice_in_dim(place, col_pos * col_span, col_span, 0)
     step_rows = 256
     k_width = 256 if 2 * pairs < LANES else 3 * wide
-    chi_spec = pl.BlockSpec((2, step_rows, col_span), lambda i, *_: (0, i, 0))
     return pl.pallas_call(
         functools.partial(update_kernel, (pairs, step_rows, col_span, wide)),
         out_shape=jax.ShapeDtypeStruct(chi0_in.shape, F32),
         grid_spec=pltpu.PrefetchScalarGridSpec(
             num_scalar_prefetch=2,
-            grid=(row_span // step_rows,),
-            in_specs=[vmem_spec, vmem_spec, chi_spec],
-            out_specs=chi_spec,
+            grid=(),
+            in_specs=[vmem_spec, vmem_spec, any_spec],
+            out_specs=any_spec,
             scratch_shapes=[
                 pltpu.VMEM((points, wide), F32),
                 pltpu.VMEM((step_rows, wide), F32),
                 pltpu.VMEM((col_span, wide), F32),
                 pltpu.VMEM((k_width, col_span), BF16),
+                pltpu.VMEM(chi0_in.shape, F32),
+                pltpu.SemaphoreType.DMA((2, row_span // step_rows)),
             ],
         ),
         compiler_params=pltpu.CompilerParams(vmem_limit_bytes=VMEM_BYTES),

time: 151 us -> 126 us (0.83)
  Pallas kernels: 139 us -> 114 us
    pallas_call x1, Pallas kernels: 70.2 us -> 56.6 us  [on_device(): pl.pallas_call(functools.partial(partial_kernel, (pairs, xb, yb, grid, ch...]
    pallas_call x1, Pallas kernels: 24.6 us -> 17.7 us  [on_device(): pl.pallas_call(functools.partial(update_kernel, (pairs, step_rows, col_sp...]
    pallas_call x1, Pallas kernels: 44.3 us -> 40.1 us  [all_sum(): pl.pallas_call(functools.partial(all_sum_kernel, parts, steps), out_shape...]
where the time goes in v3:
time: 126 us
  Pallas kernels  114 us (90%)
  other arithmetic  4.83 us (4%)
  matrix products  3.6 us (3%)
  local copies, waits for them, and re-layouts  2.58 us (2%)
    pallas_call x1, Pallas kernels, on_device(): pl.pallas_call(functools.partial(partial_kernel, (pairs, xb, yb, grid, ch...  56.6 us
    pallas_call x1, Pallas kernels, all_sum(): pl.pallas_call(functools.partial(all_sum_kernel, parts, steps), out_shape...  40.1 us
    pallas_call x1, Pallas kernels, on_device(): pl.pallas_call(functools.partial(update_kernel, (pairs, step_rows, col_sp...  17.7 us

profile of v3, /device:TPU:0, one launch (start us, length us, event | category | flops | bytes accessed | tf_op | source)
XLA Modules:
  0.0 125.5 jit_solution(1390594291191428383)
XLA Ops:
  0.0 0.6 pad_add_fusion.corner_ref
  0.6 0.9 select_reduce_fusion
  1.5 0.6 broadcast_in_dim_tile.3.weight_ref
  2.1 0.8 broadcast_select_fusion
  2.9 0.9 fusion.12
  3.8 0.1 pad_maximum_fusion
  3.9 0.7 fusion.4
  4.6 0.2 convolution_reduce_fusion
  4.8 0.1 fusion.19
  4.9 1.9 %fusion = f32[64,128]{1,0:T(8,128)S(1)} fusion(f32[128]{0:T(128)S(1)} %convolution_reduce_fusion, f32[64,128]{1,0:T(8,128)S(1)} %fusion.19, s32[64,128]{1,0:T(8,128)S(1)} %get-tuple-element.10), kind=kOutput, calls=%fused_computation.2 | convolution fusion | flops 276832256 | bytes 98816 | tf_op jit(solution)/shard_map/ab,jbk->jak/dot_general | solution.py:55
  6.8 0.6 dynamic_slice.7.col_place
  7.4 0.6 dynamic_slice.6.row_place
  8.1 0.2 fusion.7
  8.2 0.7 multiply_convert_fusion
  8.9 1.4 %fusion.3.ordered_ref = f32[256,128]{1,0:T(8,128)S(1)} fusion(bf16[8192,256]{0,1:T(8,128)(2,1)S(1)} %bitcast.29, s32[8192]{0:T(1024)S(1)} %get-tuple-element.7), kind=kOutput, calls=%fused_computation.7 | convolution fusion | flops 537919488 | bytes 4358144 | tf_op jit(solution)/shard_map/dot_general | solution.py:65
  10.3 0.0 copy-start
  10.3 0.8 slice_reduce_fusion
  11.1 0.0 copy-done
  11.1 56.6 %partial_elements.1.in_ref = f32[4096,128]{1,0:T(8,128)} custom-call(s32[32]{0:T(128)} %val_ref.1, s32[32]{0:T(128)} %cond_ref.1, s32[64]{0:T(128)} %get-tuple-element.6.first_ref, s32[64]{0:T(128)} %get-tuple-element.5.last_ref, s32[2]{0:T(128)} %pad_add_fusion.corner_ref, f32[256,128]{1,0:T(8,128)} %copy-done, bf16[288,256]{1,0:T(8,128)(2,1)} %constant.109.clone.wide_ref, ...), custom_call_target="tpu_custom_call" | custom-call | tf_op jit(solution)/shard_map/partial_elements/pallas_call | solution.py:422
  67.7 40.1 %all_sum.1.total_ref = f32[4096,128]{1,0:T(8,128)} custom-call(f32[4096,128]{1,0:T(8,128)} %partial_elements.1.in_ref), custom_call_target="tpu_custom_call" | custom-call | tf_op jit(solution)/shard_map/all_sum/pallas_call | solution.py:302
  107.8 17.7 %chi_update.1 = f32[2,2048,1024]{2,1,0:T(8,128)} custom-call(s32[2048]{0:T(1024)} %dynamic_slice.6.row_place, s32[1024]{0:T(1024)} %dynamic_slice.7.col_place, f32[4096,128]{1,0:T(8,128)} %all_sum.1.total_ref, f32[1,128]{1,0:T(1,128)} %broadcast_in_dim_tile.3.weight_ref, f32[2,2048,1024]{2,1,0:T(8,128)} %chi_ref.1), custom_call_target="tpu_custom_call" | custom-call | tf_op jit(solution)/shard_map/chi_update/pallas_call | solution.py:459
  (6 shorter events, 0.1 us)
Async XLA Ops:
  10.3 0.8 copy-start

commit v4 on v3

--- a/solution.py
+++ b/solution.py
@@ -48,7 +48,7 @@
     fold = jnp.where(flip, grid - kz, kz)
     kx = jnp.where(flip, (grid - kx) % grid, kx)
     ky = jnp.where(flip, (grid - ky) % grid, ky)
-    sign = jnp.where(flip, -1.0, 1.0).astype(F32)
+    sign = flip.astype(F32)
     bins = jnp.arange(LANES, dtype=jnp.int32)
     hot = (fold.reshape(blocks, LANES)[:, :, None] == bins).astype(BF16)
     before = (bins[:, None] > bins[None, :]).astype(BF16)
@@ -67,7 +67,7 @@
 
 
 def partial_kernel(
-    dims, val_ref, cond_ref, first_ref, last_ref, corner_ref,
+    dims, val_ref, cond_ref, first_ref, last_ref,
     ordered_ref, wide_ref, cos_ref, psi_val_ref, psi_cond_ref,
     out_ref, val_buf, cond_buf, z_buf, zz_buf, sems,
 ):
@@ -125,7 +125,9 @@
 
     lane = lax.broadcasted_iota(jnp.int32, (LANES, LANES), 1)
     u_lane = lane % 64
-    y_lane, xi_lane = u_lane // xi_count, u_lane % xi_count
+    y_lane, xi_lane = (u_lane // xi_count).astype(F32), (u_lane % xi_count).astype(F32)
+    x_corner = (lax.axis_index("row") * xb).astype(F32)
+    y_corner = (lax.axis_index("col") * yb).astype(F32)
     is_im = lane >= 64
     table = jnp.broadcast_to(cos_ref[...], (LANES, LANES))
     quarter = grid // 4
@@ -134,20 +136,21 @@
         return jnp.take_along_axis(table, steps & (grid - 1), axis=1, mode="promise_in_bounds")
 
     def elements(j, bins):
-        def column(v):
-            row = ordered_ref[pl.ds(v * chunks + j, 1), :]
+        def column(low, high):
+            row = ordered_ref[pl.ds(low * chunks + j, 1), :] + LANES * ordered_ref[pl.ds(high * chunks + j, 1), :]
             return jnp.broadcast_to(row, (LANES, LANES)).T
 
-        kx = column(0).astype(jnp.int32)
-        ky = column(1).astype(jnp.int32)
-        fold = column(2)
-        sign = column(3)
-        steps = ky * y_lane + kx * xi_lane
+        plane = column(0, 1).astype(jnp.int32)
+        kx = (plane & (LANES - 1)).astype(F32)
+        ky = (plane // LANES).astype(F32)
+        folded = column(2, 3).astype(jnp.int32)
+        fold = folded & (LANES - 1)
+        steps = (ky * y_lane + kx * xi_lane).astype(jnp.int32)
         top = cosine(steps - jnp.where(is_im, quarter, 0))
         bottom = cosine(steps + jnp.where(is_im, 0, quarter))
         left, right = [], []
         for f in bins:
-            mine = fold == f.astype(F32)
+            mine = fold == f
             high, low = split(jnp.concatenate([jnp.where(mine, top, 0.0), jnp.where(mine, bottom, 0.0)], axis=0))
             base = pl.multiple_of(jnp.minimum(f, half - 1) * 256, 256)
             left += [high, high, low]
@@ -159,8 +162,8 @@
         m_im = jnp.zeros((LANES, LANES), F32)
         for t in range(width // LANES):
             lanes = slice(t * LANES, (t + 1) * LANES)
-            x_lane = corner_ref[0] + (t * LANES + lane) // pairs * xi_count
-            steps = kx * x_lane + ky * corner_ref[1]
+            x_lane = x_corner + ((t * LANES + lane) // pairs * xi_count).astype(F32)
+            steps = (kx * x_lane + ky * y_corner).astype(jnp.int32)
             cos_p, sin_p = cosine(steps), cosine(steps - quarter)
             a_re, a_im = result[:LANES, lanes], result[LANES:, lanes]
             m_re = m_re + a_re * cos_p + a_im * sin_p
@@ -170,7 +173,7 @@
             m_re = m_re + pltpu.roll(m_re, shift, 1)
             m_im = m_im + pltpu.roll(m_im, shift, 1)
             shift //= 2
-        m_im = m_im * sign
+        m_im = jnp.where(folded < LANES, m_im, -m_im)
         if pairs < LANES:
             return (jnp.where(lane // pairs % 2 == 0, m_re, m_im),)
         return m_re, m_im
@@ -204,12 +207,12 @@
 
 
 def sum_plan(rows, mesh_rows, mesh_cols):
-    col_bits = [("col", b) for b in range(mesh_cols.bit_length() - 1)]
-    row_bits = [("row", b) for b in range(mesh_rows.bit_length() - 1)]
+    col_groups = [("col", 2**b, 2) for b in range(mesh_cols.bit_length() - 1)]
+    row_groups = [("row", 1, mesh_rows)]
     orders = (
-        col_bits + row_bits,
-        col_bits[:1] + col_bits[:0:-1] + row_bits,
-        col_bits[:1] + row_bits + col_bits[1:],
+        col_groups + row_groups,
+        col_groups[:1] + col_groups[:0:-1] + row_groups,
+        col_groups[:1] + row_groups + col_groups[1:],
     )
     unit = 8 * mesh_rows * mesh_cols
     units = rows // unit
@@ -224,91 +227,113 @@
     return parts
 
 
-def all_sum_kernel(parts, steps, in_ref, out_ref, data, land, send_sems, recv_sems):
-    def bit_of(axis, bit):
-        return lax.axis_index(axis) // 2**bit % 2
-
-    def partner(axis, bit):
-        return {axis: lax.axis_index(axis) + (1 - 2 * bit_of(axis, bit)) * 2**bit}
+def all_sum_kernel(parts, in_ref, out_ref, data, land, send_sems, recv_sems):
+    groups = parts[0][3]
+    steps = len(groups)
+
+    def place_in(group):
+        axis, stride, size = group
+        return lax.axis_index(axis) // stride % size
+
+    def peer(group, hop):
+        axis, stride, size = group
+        mine = place_in(group)
+        other = (mine + hop) % size
+        return other, {axis: lax.axis_index(axis) + (other - mine) * stride}
 
     barrier = pltpu.get_barrier_semaphore()
-    for axis, bit in parts[0][3]:
-        pl.semaphore_signal(barrier, inc=1, device_id=partner(axis, bit), device_id_type=pl.DeviceIdType.MESH)
-    pl.semaphore_wait(barrier, steps)
+    for group in groups:
+        for hop in range(1, group[2]):
+            pl.semaphore_signal(
+                barrier, inc=1, device_id=peer(group, hop)[1], device_id_type=pl.DeviceIdType.MESH
+            )
+    pl.semaphore_wait(barrier, sum(group[2] - 1 for group in groups))
 
     layout = []
     for base, rows, _, order in parts:
         here, size, spots, lands = base, rows, [], base
-        for axis, bit in order:
-            size //= 2
-            side = bit_of(axis, bit)
-            keep = pl.multiple_of(here + side * size, 8)
-            away = pl.multiple_of(here + (1 - side) * size, 8)
-            spots.append((keep, away, size, lands))
-            lands += size
-            here = keep
+        for group in order:
+            size //= group[2]
+            spots.append((here, size, lands))
+            lands += size * (group[2] - 1)
+            here = pl.multiple_of(here + place_in(group) * size, 8)
         layout.append(spots)
 
-    def copy_of(k, step):
-        order = parts[k][3]
-        if step < steps:
-            keep, away, size, lands = layout[k][step]
-            source = (in_ref if step == 0 else data).at[pl.ds(away, size)]
-            target = land.at[pl.ds(lands, size)]
-            axis, bit = order[step]
-        else:
-            back = 2 * steps - 1 - step
-            keep, away, size, lands = layout[k][back]
-            source = target = out_ref.at[pl.ds(keep, size)]
-            axis, bit = order[back]
-        return pltpu.make_async_remote_copy(
-            src_ref=source,
-            dst_ref=target,
-            send_sem=send_sems.at[k, step],
-            recv_sem=recv_sems.at[k, step],
-            device_id=partner(axis, bit),
-            device_id_type=pl.DeviceIdType.MESH,
-        )
+    def copies_of(k, step):
+        back = step if step < steps else 2 * steps - 1 - step
+        here, size, lands = layout[k][back]
+        group = parts[k][3][back]
+        found = []
+        for hop in range(1, group[2]):
+            other, device = peer(group, hop)
+            if step < steps:
+                away = pl.multiple_of(here + other * size, 8)
+                source = (in_ref if step == 0 else data).at[pl.ds(away, size)]
+                target = land.at[pl.ds(lands + (hop - 1) * size, size)]
+            else:
+                keep = pl.multiple_of(here + place_in(group) * size, 8)
+                source = target = out_ref.at[pl.ds(keep, size)]
+            found.append(
+                pltpu.make_async_remote_copy(
+                    src_ref=source,
+                    dst_ref=target,
+                    send_sem=send_sems.at[k, step, hop - 1],
+                    recv_sem=recv_sems.at[k, step, hop - 1],
+                    device_id=device,
+                    device_id_type=pl.DeviceIdType.MESH,
+                )
+            )
+        return found
 
     def add(k, step):
-        keep, _, size, lands = layout[k][step]
+        here, size, lands = layout[k][step]
+        group = parts[k][3][step]
+        keep = here + place_in(group) * size
         source = in_ref if step == 0 else data
         target = out_ref if step == steps - 1 else data
-        piece = 8 * parts[k][2] * 2 ** min(steps - step - 1, 2)
+        piece = min(size, 32 * parts[k][2])
 
         @pl.loop(0, size // piece)
         def _(i):
             spot = pl.ds(pl.multiple_of(keep + i * piece, 8), piece)
-            target[spot, :] = source[spot, :] + land[pl.ds(pl.multiple_of(lands + i * piece, 8), piece), :]
+            value = source[spot, :]
+            for hop in range(1, group[2]):
+                start = lands + (hop - 1) * size + i * piece
+                value = value + land[pl.ds(pl.multiple_of(start, 8), piece), :]
+            target[spot, :] = value
 
     for k in range(len(parts)):
-        copy_of(k, 0).start()
+        for copy in copies_of(k, 0):
+            copy.start()
     for step in range(2 * steps):
         for k in range(len(parts)):
-            copy_of(k, step).wait_recv()
+            for copy in copies_of(k, step):
+                copy.wait_recv()
             if step < steps:
                 add(k, step)
             if step < 2 * steps - 1:
-                copy_of(k, step + 1).start()
+                for copy in copies_of(k, step + 1):
+                    copy.start()
     for step in range(2 * steps):
         for k in range(len(parts)):
-            copy_of(k, step).wait_send()
+            for copy in copies_of(k, step):
+                copy.wait_send()
 
 
 def all_sum(value, mesh_rows, mesh_cols):
     parts = sum_plan(value.shape[0], mesh_rows, mesh_cols)
-    steps = len(parts[0][3])
+    slots = (len(parts), 2 * len(parts[0][3]), max(group[2] for group in parts[0][3]) - 1)
     vmem_spec = pl.BlockSpec(memory_space=pltpu.VMEM)
     return pl.pallas_call(
-        functools.partial(all_sum_kernel, parts, steps),
+        functools.partial(all_sum_kernel, parts),
         out_shape=jax.ShapeDtypeStruct(value.shape, F32),
         in_specs=[vmem_spec],
         out_specs=vmem_spec,
         scratch_shapes=[
             pltpu.VMEM(value.shape, F32),
             pltpu.VMEM(value.shape, F32),
-            pltpu.SemaphoreType.DMA((len(parts), 2 * steps)),
-            pltpu.SemaphoreType.DMA((len(parts), 2 * steps)),
+            pltpu.SemaphoreType.DMA(slots),
+            pltpu.SemaphoreType.DMA(slots),
         ],
         compiler_params=pltpu.CompilerParams(
             collective_id=0, has_side_effects=True, vmem_limit_bytes=VMEM_BYTES
@@ -318,7 +343,7 @@
 
 
 def update_kernel(
-    dims, row_place, col_place, total_ref, weight_ref, chi_ref, out_ref,
+    dims, place, val_ref, cond_ref, eps_val_ref, eps_cond_ref, total_ref, chi_ref, out_ref,
     m_ref, row_buf, col_buf, right_buf, chi_buf, sems,
 ):
     pairs, step_rows, cols, wide = dims
@@ -336,7 +361,7 @@
     def _(step):
         arrival(step).start()
 
-    def gather(place, base, buf, count):
+    def gather(base, buf, count):
         @pl.loop(0, count // 16)
         def _(i):
             found = [m_ref[pl.ds(place[base + i * 16 + k], 1), :] for k in range(16)]
@@ -362,6 +387,13 @@
             return jnp.concatenate([high, jnp.where(keep, low.astype(F32), 0.0).astype(BF16)], axis=0)
         return jnp.concatenate([high, high, low], axis=0)
 
+    pair_lane = lax.broadcasted_iota(jnp.int32, (8, wide), 1) % pairs
+
+    def set_gap(p, gaps):
+        return jnp.where(pair_lane == p, eps_cond_ref[cond_ref[p]] - eps_val_ref[val_ref[p]], gaps)
+
+    gaps = lax.fori_loop(0, pairs, set_gap, jnp.ones((8, wide), F32))
+    weight = (-6.0 / (math.sqrt(pairs) * gaps))[:1]
     packed = total_ref.shape[0]
     piece = 64
 
@@ -379,13 +411,13 @@
                     shift *= 2
             m_ref[pl.ds(pl.multiple_of(q * packed + i * piece, piece), piece), :] = part
 
-    gather(col_place, 0, col_buf, cols)
+    gather(lax.axis_index("col") * cols, col_buf, cols)
     right_buf[...] = join_right(col_buf[...].T)
 
     @pl.loop(0, steps)
     def _(step):
-        gather(row_place, step * step_rows, row_buf, step_rows)
-        left = row_buf[...] * weight_ref[...]
+        gather((lax.axis_index("row") * steps + step) * step_rows, row_buf, step_rows)
+        left = row_buf[...] * weight
         lane = lax.broadcasted_iota(jnp.int32, left.shape, 1)
         turned = pltpu.roll(left, wide - pairs, 1)
         turned = jnp.where(lane // pairs % 2 == 0, turned, -turned)
@@ -407,10 +439,8 @@
     bands_c = psi_cond.shape[0]
     points = gmap.shape[0]
     chunks = points // LANES
-    row_pos, col_pos = lax.axis_index("row"), lax.axis_index("col")
     place, ordered = sort_points(gmap, grid)
     fold = ordered[2 * chunks : 3 * chunks].astype(jnp.int32)
-    corner = jnp.stack([row_pos * xb, col_pos * yb]).astype(jnp.int32)
     z_wide = z_tables(grid)
     cos_row = jnp.asarray(np.cos(np.arange(grid) * (2.0 * math.pi / grid))[None, :], F32)
     wide = max(LANES, 2 * pairs)
@@ -423,7 +453,7 @@
         functools.partial(partial_kernel, (pairs, xb, yb, grid, chunks)),
         out_shape=jax.ShapeDtypeStruct((points * 2 * pairs // wide, wide), F32),
         grid_spec=pltpu.PrefetchScalarGridSpec(
-            num_scalar_prefetch=5,
+            num_scalar_prefetch=4,
             grid=(),
             in_specs=[vmem_spec] * 3 + [any_spec] * 2,
             out_specs=vmem_spec,
@@ -438,31 +468,22 @@
         compiler_params=pltpu.CompilerParams(vmem_limit_bytes=VMEM_BYTES),
         name="partial_elements",
     )(
-        val_index, cond_index, fold[:, 0], fold[:, LANES - 1], corner,
+        val_index, cond_index, fold[:, 0], fold[:, LANES - 1],
         ordered, z_wide, cos_row,
         psi_val.reshape(bands_v, rows, grid), psi_cond.reshape(bands_c, rows, grid),
     )
     total = all_sum(partial, lax.axis_size("row"), lax.axis_size("col"))
 
-    val_hot = val_index[:, None] == jnp.arange(bands_v, dtype=jnp.int32)[None, :]
-    cond_hot = cond_index[:, None] == jnp.arange(bands_c, dtype=jnp.int32)[None, :]
-    energy_v = jnp.sum(jnp.where(val_hot, eps_val[None, :], 0.0), axis=1)
-    energy_c = jnp.sum(jnp.where(cond_hot, eps_cond[None, :], 0.0), axis=1)
-    weight = -6.0 / (math.sqrt(pairs) * (energy_c - energy_v))
-    weight = jnp.tile(weight, wide // pairs)[None, :]
-
     _, row_span, col_span = chi0_in.shape
-    row_place = lax.dynamic_slice_in_dim(place, row_pos * row_span, row_span, 0)
-    col_place = lax.dynamic_slice_in_dim(place, col_pos * col_span, col_span, 0)
     step_rows = 256
     k_width = 256 if 2 * pairs < LANES else 3 * wide
     return pl.pallas_call(
         functools.partial(update_kernel, (pairs, step_rows, col_span, wide)),
         out_shape=jax.ShapeDtypeStruct(chi0_in.shape, F32),
         grid_spec=pltpu.PrefetchScalarGridSpec(
-            num_scalar_prefetch=2,
+            num_scalar_prefetch=5,
             grid=(),
-            in_specs=[vmem_spec, vmem_spec, any_spec],
+            in_specs=[vmem_spec, any_spec],
             out_specs=any_spec,
             scratch_shapes=[
                 pltpu.VMEM((points, wide), F32),
@@ -475,7 +496,7 @@
         ),
         compiler_params=pltpu.CompilerParams(vmem_limit_bytes=VMEM_BYTES),
         name="chi_update",
-    )(row_place, col_place, total, weight, chi0_in)
+    )(place, val_index, cond_index, eps_val, eps_cond, total, chi0_in)
 
 
 def solution(mesh):

time: 126 us -> 121 us (0.960)
  Pallas kernels: 114 us -> 112 us
  local copies, waits for them, and re-layouts: 2.58 us -> 0.77 us
    pallas_call x1, Pallas kernels: 56.6 us -> 53.6 us  [on_device(): pl.pallas_call(functools.partial(partial_kernel, (pairs, xb, yb, grid, ch...]
where the time goes in v4:
time: 121 us
  Pallas kernels  112 us (93%)
  other arithmetic  3.96 us (3%)
  matrix products  3.6 us (3%)
    pallas_call x1, Pallas kernels, on_device(): pl.pallas_call(functools.partial(partial_kernel, (pairs, xb, yb, grid, ch...  53.6 us
    pallas_call x1, Pallas kernels, all_sum(): pl.pallas_call(functools.partial(all_sum_kernel, parts), out_shape=jax.Sh...  40.2 us
    pallas_call x1, Pallas kernels, on_device(): pl.pallas_call(functools.partial(update_kernel, (pairs, step_rows, col_sp...  18.3 us

profile of v4, /device:TPU:0, one launch (start us, length us, event | category | flops | bytes accessed | tf_op | source)
XLA Modules:
  0.0 120.5 jit_solution(2034068176242766426)
XLA Ops:
  0.0 0.8 fusion.27
  0.8 0.9 fusion.12
  1.7 0.1 pad_maximum_fusion
  1.8 0.7 fusion.4
  2.5 0.2 convolution_reduce_fusion
  2.7 0.1 fusion.19
  2.8 1.9 %fusion = f32[64,128]{1,0:T(8,128)S(1)} fusion(f32[128]{0:T(128)S(1)} %convolution_reduce_fusion, f32[64,128]{1,0:T(8,128)S(1)} %fusion.19, s32[64,128]{1,0:T(8,128)S(1)} %get-tuple-element.10), kind=kOutput, calls=%fused_computation.2 | convolution fusion | flops 276832256 | bytes 98816 | tf_op jit(solution)/shard_map/ab,jbk->jak/dot_general | solution.py:55
  4.7 0.6 convert_bitcast_fusion.place
  5.4 0.2 fusion.7
  5.5 0.7 multiply_convert_fusion
  6.2 1.4 %fusion.3.ordered_ref = f32[256,128]{1,0:T(8,128)S(1)} fusion(bf16[8192,256]{0,1:T(8,128)(2,1)S(1)} %bitcast.27, s32[8192]{0:T(1024)S(1)} %get-tuple-element.7), kind=kOutput, calls=%fused_computation.7 | convolution fusion | flops 537919488 | bytes 4358144 | tf_op jit(solution)/shard_map/dot_general | solution.py:65
  7.6 0.0 copy-start
  7.6 0.8 slice_reduce_fusion
  8.4 0.0 copy-done
  8.4 53.6 %partial_elements.1.in_ref = f32[4096,128]{1,0:T(8,128)} custom-call(s32[32]{0:T(128)} %val_ref.3, s32[32]{0:T(128)} %cond_ref.3, s32[64]{0:T(128)} %get-tuple-element.6.first_ref, s32[64]{0:T(128)} %get-tuple-element.5.last_ref, f32[256,128]{1,0:T(8,128)} %copy-done, bf16[288,256]{1,0:T(8,128)(2,1)} %constant.82.clone.wide_ref, ...), custom_call_target="tpu_custom_call" | custom-call | tf_op jit(solution)/shard_map/partial_elements/pallas_call | solution.py:452
  62.0 40.2 %all_sum.1.total_ref = f32[4096,128]{1,0:T(8,128)} custom-call(f32[4096,128]{1,0:T(8,128)} %partial_elements.1.in_ref), custom_call_target="tpu_custom_call" | custom-call | tf_op jit(solution)/shard_map/all_sum/pallas_call | solution.py:327
  102.2 18.3 %chi_update.1 = f32[2,2048,1024]{2,1,0:T(8,128)} custom-call(s32[8192]{0:T(1024)} %convert_bitcast_fusion.place, s32[32]{0:T(128)} %val_ref.3, s32[32]{0:T(128)} %cond_ref.3, f32[64]{0:T(128)} %eps_val_ref.1, f32[64]{0:T(128)} %eps_cond_ref.1, f32[4096,128]{1,0:T(8,128)} %all_sum.1.total_ref, f32[2,2048,1024]{2,1,0:T(8,128)} %chi_ref.1), custom_call_target="tpu_custom_call" | custom-call | tf_op jit(solution)/shard_map/chi_update/pallas_call | solution.py:480
  (3 shorter events, 0.1 us)
Async XLA Ops:
  7.6 0.8 copy-start

commit v5 on v4

--- a/solution.py
+++ b/solution.py
@@ -78,42 +78,48 @@
     width = xo_count * pairs
     half = grid // 2 + 1
 
-    def copies(p):
-        spot = pl.ds(pl.multiple_of(p * (rows + 8), 8), rows)
+    def copies(p, part):
+        here = pl.ds(part * (rows // 2), rows // 2)
+        spot = pl.ds(pl.multiple_of(p * (rows + 8) + part * (rows // 2), 8), rows // 2)
         return (
-            pltpu.make_async_copy(psi_val_ref.at[val_ref[p]], val_buf.at[spot], sems.at[0, p]),
-            pltpu.make_async_copy(psi_cond_ref.at[cond_ref[p]], cond_buf.at[spot], sems.at[1, p]),
+            pltpu.make_async_copy(psi_val_ref.at[val_ref[p], here], val_buf.at[spot], sems.at[0, part, p]),
+            pltpu.make_async_copy(psi_cond_ref.at[cond_ref[p], here], cond_buf.at[spot], sems.at[1, part, p]),
         )
 
-    @pl.loop(0, pairs)
-    def _(p):
-        for copy in copies(p):
-            copy.start()
-
-    @pl.loop(0, pairs)
-    def _(p):
-        for copy in copies(p):
-            copy.wait()
-
-    def transform(u):
-        y, xi = u // xi_count, u % xi_count
+    def transform(y, xi):
         parts = []
         for xo in range(xo_count):
-            spot = pl.ds((xo * xi_count + xi) * yb + y, pairs, stride=rows + 8)
+            spot = pl.ds((xi * xo_count + xo) * yb + y, pairs, stride=rows + 8)
             parts.append(val_buf[spot, :] * cond_buf[spot, :])
         high, low = split(jnp.concatenate(parts, axis=0))
         both = jnp.concatenate([high, low], axis=1)
         z = lax.dot_general(wide_ref[...], both, NT, preferred_element_type=F32)
         return z[: 2 * ROW_PAD] + z[2 * ROW_PAD :]
 
-    @pl.loop(0, 16)
-    def _(i):
-        results = [transform(i * 4 + k) for k in range(4)]
-        for k, z in enumerate(results):
-            for t in range(width // LANES):
-                lanes = slice(t * LANES, (t + 1) * LANES)
-                z_buf[t, pl.ds(i * 4 + k, ROW_PAD, stride=Z_STRIDE), :] = z[:ROW_PAD, lanes]
-                z_buf[t, pl.ds(64 + i * 4 + k, ROW_PAD, stride=Z_STRIDE), :] = z[ROW_PAD:, lanes]
+    for part in range(2):
+
+        @pl.loop(0, pairs)
+        def _(p):
+            for copy in copies(p, part):
+                copy.start()
+
+    for part in range(2):
+
+        @pl.loop(0, pairs)
+        def _(p):
+            for copy in copies(p, part):
+                copy.wait()
+
+        @pl.loop(0, 8)
+        def _(i):
+            spots = [((i * 4 + k) % yb, part * (xi_count // 2) + (i * 4 + k) // yb) for k in range(4)]
+            results = [transform(y, xi) for y, xi in spots]
+            for (y, xi), z in zip(spots, results):
+                u = y * xi_count + xi
+                for t in range(width // LANES):
+                    lanes = slice(t * LANES, (t + 1) * LANES)
+                    z_buf[t, pl.ds(u, ROW_PAD, stride=Z_STRIDE), :] = z[:ROW_PAD, lanes]
+                    z_buf[t, pl.ds(64 + u, ROW_PAD, stride=Z_STRIDE), :] = z[ROW_PAD:, lanes]
 
     @pl.loop(0, half)
     def _(kz):
@@ -125,7 +131,7 @@
 
     lane = lax.broadcasted_iota(jnp.int32, (LANES, LANES), 1)
     u_lane = lane % 64
-    y_lane, xi_lane = (u_lane // xi_count).astype(F32), (u_lane % xi_count).astype(F32)
+    y_lane, xi_lane = (u_lane // xi_count).astype(F32), (u_lane % xi_count * xo_count).astype(F32)
     x_corner = (lax.axis_index("row") * xb).astype(F32)
     y_corner = (lax.axis_index("col") * yb).astype(F32)
     is_im = lane >= 64
@@ -162,7 +168,7 @@
         m_im = jnp.zeros((LANES, LANES), F32)
         for t in range(width // LANES):
             lanes = slice(t * LANES, (t + 1) * LANES)
-            x_lane = x_corner + ((t * LANES + lane) // pairs * xi_count).astype(F32)
+            x_lane = x_corner + ((t * LANES + lane) // pairs).astype(F32)
             steps = (kx * x_lane + ky * y_corner).astype(jnp.int32)
             cos_p, sin_p = cosine(steps), cosine(steps - quarter)
             a_re, a_im = result[:LANES, lanes], result[LANES:, lanes]
@@ -362,12 +368,12 @@
         arrival(step).start()
 
     def gather(base, buf, count):
-        @pl.loop(0, count // 16)
+        @pl.loop(0, count // 64)
         def _(i):
-            found = [m_ref[pl.ds(place[base + i * 16 + k], 1), :] for k in range(16)]
-            for half in range(2):
-                spot = pl.ds(pl.multiple_of(i * 16 + half * 8, 8), 8)
-                buf[spot, :] = jnp.concatenate(found[half * 8 : half * 8 + 8], axis=0)
+            found = [m_ref[pl.ds(place[base + i * 64 + k], 1), :] for k in range(64)]
+            for tile in range(8):
+                spot = pl.ds(pl.multiple_of(i * 64 + tile * 8, 8), 8)
+                buf[spot, :] = jnp.concatenate(found[tile * 8 : tile * 8 + 8], axis=0)
 
     def join(value):
         high, low = split(value)
@@ -458,11 +464,11 @@
             in_specs=[vmem_spec] * 3 + [any_spec] * 2,
             out_specs=vmem_spec,
             scratch_shapes=[
-                pltpu.VMEM((pairs * (rows + 8), grid), F32),
-                pltpu.VMEM((pairs * (rows + 8), grid), F32),
-                pltpu.VMEM((width // LANES, ROW_PAD * Z_STRIDE, LANES), F32),
+                pltpu.VMEM(((pairs + 1) * (rows + 8), grid), F32),
+                pltpu.VMEM(((pairs + 1) * (rows + 8), grid), F32),
+                pltpu.VMEM((width // LANES, (ROW_PAD + 1) * Z_STRIDE, LANES), F32),
                 pltpu.VMEM(((grid // 2 + 1) * 256, width), BF16),
-                pltpu.SemaphoreType.DMA((2, pairs)),
+                pltpu.SemaphoreType.DMA((2, 2, pairs)),
             ],
         ),
         compiler_params=pltpu.CompilerParams(vmem_limit_bytes=VMEM_BYTES),

time: 121 us -> 121 us (level)
  no operation moved by 1% of the time
where the time goes in v5:
time: 121 us; the launch traced here: 120 us
  Pallas kernels  112 us (93%)
  other arithmetic  3.96 us (3%)
  matrix products  3.6 us (3%)
    pallas_call x1, Pallas kernels, on_device(): pl.pallas_call(functools.partial(partial_kernel, (pairs, xb, yb, grid, ch...  54.3 us
    pallas_call x1, Pallas kernels, all_sum(): pl.pallas_call(functools.partial(all_sum_kernel, parts), out_shape=jax.Sh...  40.2 us
    pallas_call x1, Pallas kernels, on_device(): pl.pallas_call(functools.partial(update_kernel, (pairs, step_rows, col_sp...  17.5 us

profile of v5, /device:TPU:0, one launch (start us, length us, event | category | flops | bytes accessed | tf_op | source)
XLA Modules:
  0.0 120.4 jit_solution(16885031903698333469)
XLA Ops:
  0.0 0.8 fusion.27
  0.8 0.9 fusion.12
  1.7 0.1 pad_maximum_fusion
  1.8 0.7 fusion.4
  2.5 0.2 convolution_reduce_fusion
  2.7 0.1 fusion.19
  2.8 1.9 %fusion = f32[64,128]{1,0:T(8,128)S(1)} fusion(f32[128]{0:T(128)S(1)} %convolution_reduce_fusion, f32[64,128]{1,0:T(8,128)S(1)} %fusion.19, s32[64,128]{1,0:T(8,128)S(1)} %get-tuple-element.10), kind=kOutput, calls=%fused_computation.2 | convolution fusion | flops 276832256 | bytes 98816 | tf_op jit(solution)/shard_map/ab,jbk->jak/dot_general | solution.py:55
  4.7 0.6 convert_bitcast_fusion.place
  5.4 0.2 fusion.7
  5.5 0.7 multiply_convert_fusion
  6.2 1.4 %fusion.3.ordered_ref = f32[256,128]{1,0:T(8,128)S(1)} fusion(bf16[8192,256]{0,1:T(8,128)(2,1)S(1)} %bitcast.27, s32[8192]{0:T(1024)S(1)} %get-tuple-element.7), kind=kOutput, calls=%fused_computation.7 | convolution fusion | flops 537919488 | bytes 4358144 | tf_op jit(solution)/shard_map/dot_general | solution.py:65
  7.6 0.0 copy-start
  7.6 0.8 slice_reduce_fusion
  8.4 0.0 copy-done
  8.4 54.3 %partial_elements.1.in_ref = f32[4096,128]{1,0:T(8,128)} custom-call(s32[32]{0:T(128)} %val_ref.3, s32[32]{0:T(128)} %cond_ref.3, s32[64]{0:T(128)} %get-tuple-element.6.first_ref, s32[64]{0:T(128)} %get-tuple-element.5.last_ref, f32[256,128]{1,0:T(8,128)} %copy-done, bf16[288,256]{1,0:T(8,128)(2,1)} %constant.82.clone.wide_ref, ...), custom_call_target="tpu_custom_call" | custom-call | tf_op jit(solution)/shard_map/partial_elements/pallas_call | solution.py:458
  62.7 40.2 %all_sum.1.total_ref = f32[4096,128]{1,0:T(8,128)} custom-call(f32[4096,128]{1,0:T(8,128)} %partial_elements.1.in_ref), custom_call_target="tpu_custom_call" | custom-call | tf_op jit(solution)/shard_map/all_sum/pallas_call | solution.py:333
  102.9 17.5 %chi_update.1 = f32[2,2048,1024]{2,1,0:T(8,128)} custom-call(s32[8192]{0:T(1024)} %convert_bitcast_fusion.place, s32[32]{0:T(128)} %val_ref.3, s32[32]{0:T(128)} %cond_ref.3, f32[64]{0:T(128)} %eps_val_ref.1, f32[64]{0:T(128)} %eps_cond_ref.1, f32[4096,128]{1,0:T(8,128)} %all_sum.1.total_ref, f32[2,2048,1024]{2,1,0:T(8,128)} %chi_ref.1), custom_call_target="tpu_custom_call" | custom-call | tf_op jit(solution)/shard_map/chi_update/pallas_call | solution.py:486
  (3 shorter events, 0.1 us)
Async XLA Ops:
  7.6 0.8 copy-start
